TPU v7x, 32 devices: a whole 2x2x4 slice. The times are simulated.
32 devices in a mesh: rows: 8 (over z, x), cols: 4 (over y, core).
Axes of the slice: x: 2, y: 2, z: 4, core: 2. Of those that a mesh axis runs over, the one named last changes fastest.
Arguments:
- graph_tiles: bfloat16 [128, 17, 128, 128], P('rows'), as said below
- tile_column: int32 [128, 17], P('rows'), may hold values from 0 to 127, as said below
- tile_count: int32 [128], P('rows'), may hold values from 1 to 17, as said below
- class_label: int32 [16384], P('rows'), may hold values from 0 to 999
- confidence: float32 [16384], P('rows'), may hold values from 0.2 to 1
- class_weight: float32 [1000], P('cols'), may hold values from 0.25 to 4
Outputs:
- scores: float32 [16384, 1000], P('rows', 'cols')
- residual: float32 [16384, 1000], P('rows', 'cols')
Inputs may be any that keep to these rules, and one draw needn't show every extreme that they name: `tile_column`: Block-row i's live tiles lie in distinct block-columns (i + d) mod 128 with |d| <= 8; block-row i has a live tile in block-column j exactly when block-row j has one in block-column i. `tile_count`: slots at and beyond a block-row's count are unused. `graph_tiles`: the matrix S assembled from the live tiles is symmetric: the tile of block-row i in block-column j is the transpose of the tile of block-row j in block-column i. Entries of a live tile of block-row i in block-column j lie between 0 and 1 / (128 * sqrt(tile_count[i] * tile_count[j])).
All inputs are finite; a program needn't handle non-finite values.
Results may differ from a plain program's by a relative error of at most 0.003.
Values may be sent and summed in bfloat16 or wider, within the bound.
A program may use at most 128 MiB of HBM per device.

v0:
```python
import jax
import jax.numpy as jnp
from jax import lax
from jax.sharding import PartitionSpec as P

ITERS = 3


damping = 0.99
smoothing = 0.1


def padded(cells, sides, width):
    for axis, dim in sides:
        count = lax.axis_size(axis)
        head = lax.slice_in_dim(cells, 0, width, axis=dim)
        tail = lax.slice_in_dim(cells, cells.shape[dim] - width, cells.shape[dim], axis=dim)
        cells = jnp.concatenate(
            [
                lax.ppermute(tail, axis, [(i, (i + 1) % count) for i in range(count)]),
                cells,
                lax.ppermute(head, axis, [((i + 1) % count, i) for i in range(count)]),
            ],
            axis=dim,
        )
    return cells


def body(graph_tiles, tile_column, tile_count, class_label, confidence, class_weight):
    block_rows = graph_tiles.shape[0]
    slot_count = graph_tiles.shape[1]
    block_size = graph_tiles.shape[2]
    class_dev = class_weight.shape[0]
    half_span = block_rows // 2
    total_blocks = block_rows * lax.axis_size("rows")
    first_row = lax.axis_index("rows") * block_rows - half_span
    local_col = jnp.mod(tile_column - first_row, total_blocks)
    live_slot = jnp.arange(slot_count, dtype=jnp.int32)[None, :] < tile_count[:, None]
    class_ids = lax.axis_index("cols") * class_dev + jnp.arange(class_dev, dtype=jnp.int32)
    onehot = (class_label[:, None] == class_ids[None, :]).astype(jnp.float32)
    prior_labels = (
        confidence[:, None]
        * class_weight[None, :]
        * ((1.0 - smoothing) * onehot + smoothing / (class_dev * lax.axis_size("cols")))
    )
    zero_half = jnp.zeros((), jnp.bfloat16)

    def squares(residual):
        return lax.psum(jnp.sum(residual * residual, axis=0), "rows")

    solution = jnp.zeros_like(prior_labels)
    residual = prior_labels
    direction = prior_labels
    norm_now = squares(residual)
    for step in range(ITERS):
        extended = padded(direction.astype(jnp.bfloat16), (("rows", 0),), half_span * block_size)
        blocks = extended.reshape(block_rows + 2 * half_span, block_size, class_dev)
        picked = blocks[local_col]
        picked = jnp.where(live_slot[:, :, None, None], picked, zero_half)
        product_sum = jnp.einsum(
            "rkij,rkjc->ric", graph_tiles, picked, preferred_element_type=jnp.float32
        )
        applied = direction - damping * product_sum.reshape(block_rows * block_size, class_dev)
        curve_sum = lax.psum(jnp.sum(direction * applied, axis=0), "rows")
        step_size = norm_now / curve_sum
        solution = solution + step_size[None, :] * direction
        residual = residual - step_size[None, :] * applied
        norm_next = squares(residual)
        direction = residual + (norm_next / norm_now)[None, :] * direction
        norm_now = norm_next
    row_squares = lax.psum(jnp.sum(solution * solution, axis=1), "cols")
    length = jnp.sqrt(row_squares + 1e-06)
    return (solution / length[:, None], residual)


def solution(mesh):
    placed = (
        P("rows", None, None, None),
        P("rows", None),
        P("rows"),
        P("rows"),
        P("rows"),
        P("cols"),
    )
    return jax.shard_map(
        body,
        mesh=mesh,
        in_specs=placed,
        out_specs=(P("rows", "cols"), P("rows", "cols")),
        check_vma=False,
    )
```

profile of v0, /device:TPU:0, one launch (start us, length us, event | category | flops | bytes accessed | tf_op | source)
XLA Modules:
  0.0 256.3 jit_solution(3339807034369957189)
XLA Ops:
  0.6 0.0 copy-start.7
  0.6 0.0 copy-start.8
  0.7 1.5 multiply_reduce_fusion.5
  2.1 0.1 fusion.34
  2.2 3.0 %collective-permute-start = (bf16[1024,250]{1,0:T(8,128)(2,1)S(1)}, bf16[1024,250]{1,0:T(8,128)(2,1)S(1)}, u32[]{:S(2)}, u32[]{:S(2)}) collective-permute-start(bf16[1024,250]{1,0:T(8,128)(2,1)S(1)} %get-tuple-element.10), channel_id=1, source_target_pairs={{0,4},{4,8},{8,12},{12,16},{16,20},{20,24},{24,28},{28,0},{1,5},{5... | collective-permute-start | bytes 1536008 | tf_op jit(solution)/shard_map/ppermute | solution.py:20
  5.2 3.1 %collective-permute-start.1 = (bf16[1024,250]{1,0:T(8,128)(2,1)S(1)}, bf16[1024,250]{1,0:T(8,128)(2,1)}, u32[]{:S(2)}, u32[]{:S(2)}) collective-permute-start(bf16[1024,250]{1,0:T(8,128)(2,1)S(1)} %get-tuple-element.11), channel_id=1, source_target_pairs={{4,0},{8,4},{12,8},{16,12},{20,16},{24,20},{28,24},{0,28},{5,1},{9... | collective-permute-start | bytes 1536008 | tf_op jit(solution)/shard_map/ppermute | solution.py:22
  8.3 0.0 copy-done.7
  8.3 0.1 reshape.234
  8.4 0.1 iota_compare_fusion
  8.5 19.1 %collective-permute-done = bf16[1024,250]{1,0:T(8,128)(2,1)S(1)} collective-permute-done((bf16[1024,250]{1,0:T(8,128)(2,1)S(1)}, bf16[1024,250]{1,0:T(8,128)(2,1)S(1)}, u32[]{:S(2)}, u32[]{:S(2)}) %collective-permute-start) | collective-permute-done | bytes 512032 | tf_op jit(solution)/shard_map/ppermute | solution.py:20
  27.6 0.8 copy-done.3
  28.4 1.5 collective-permute-done.1
  29.9 1.5 pad_maximum_fusion
  31.5 0.0 copy-start.4
  31.5 0.0 copy-start.5
  31.5 0.0 copy-start.6
  31.5 10.4 %gather_fusion = bf16[272,128,250]{2,1,0:T(8,128)(2,1)} fusion(bf16[32,128,250]{2,1,0:T(8,128)(2,1)S(1)} %bitcast.97, s32[1024]{0:T(1024)S(1)} %pad_clamp_fusion), kind=kCustom, calls=%fused_computation | custom fusion | bytes 34817088 | tf_op jit(solution)/shard_map/gather | solution.py:58
  41.9 10.4 %multiply_reduce_fusion.4 = (f32[250]{0:T(256)S(1)}, f32[16,250,128]{1,2,0:T(8,128)S(1)}) fusion(s32[250]{0:T(256)S(1)} %iota_add_fusion, s32[16,128]{1,0:T(8,128)S(1)} %bitcast.102, f32[250]{0:T(256)S(1)} %copy-done.6, f32[16,128]{1,0:T(8,128)S(1)} %bitcast.108, bf16[16,17,128,128]{3,2,1,0:T(8,128)(2,1)} %param.6, ...), kind=kOutput, calls=%fused_computation.45 | convolution fusion | flops 2241535744 | bytes 28388552 | tf_op jit(solution)/shard_map/rkij,rkjc->ric/dot_general | solution.py:60
  52.3 0.0 copy-start
  52.4 21.1 %all-reduce = (f32[250]{0:T(256)S(1)}, f32[250]{0:T(256)S(1)}) all-reduce(f32[250]{0:T(256)S(1)} %get-tuple-element.12, f32[250]{0:T(256)S(1)} %get-tuple-element.14), channel_id=1, replica_groups=mesh['rows'=8,'cols'=4] {'rows'}, use_global_device_ids=true, to_apply=%region_1.2 | all-reduce | flops 500 | bytes 4000 | tf_op jit(solution)/shard_map/psum | solution.py:49
  73.5 0.9 multiply_reduce_fusion.3
  74.4 17.4 %psum.51 = f32[250]{0:T(256)S(1)} all-reduce(f32[250]{0:T(256)S(1)} %multiply_reduce_fusion.3), channel_id=1, replica_groups=mesh['rows'=8,'cols'=4] {'rows'}, use_global_device_ids=true, to_apply=%region_5.6 | all-reduce | flops 250 | bytes 2000 | tf_op jit(solution)/shard_map/psum | solution.py:49
  91.8 1.1 fusion.31
  92.9 0.0 copy-done
  92.9 0.1 fusion.33
  93.0 4.2 %collective-permute-start.2 = (bf16[1024,250]{1,0:T(8,128)(2,1)S(1)}, bf16[1024,250]{1,0:T(8,128)(2,1)S(1)}, u32[]{:S(2)}, u32[]{:S(2)}) collective-permute-start(bf16[1024,250]{1,0:T(8,128)(2,1)S(1)} %get-tuple-element.8), channel_id=1, source_target_pairs={{0,4},{4,8},{8,12},{12,16},{16,20},{20,24},{24,28},{28,0},{1,5},{5... | collective-permute-start | bytes 1536008 | tf_op jit(solution)/shard_map/ppermute | solution.py:20
  97.1 4.1 %collective-permute-start.3 = (bf16[1024,250]{1,0:T(8,128)(2,1)S(1)}, bf16[1024,250]{1,0:T(8,128)(2,1)S(1)}, u32[]{:S(2)}, u32[]{:S(2)}) collective-permute-start(bf16[1024,250]{1,0:T(8,128)(2,1)S(1)} %get-tuple-element.9), channel_id=1, source_target_pairs={{4,0},{8,4},{12,8},{16,12},{20,16},{24,20},{28,24},{0,28},{5,1},{9... | collective-permute-start | bytes 1536008 | tf_op jit(solution)/shard_map/ppermute | solution.py:22
  101.3 8.2 %collective-permute-done.2 = bf16[1024,250]{1,0:T(8,128)(2,1)S(1)} collective-permute-done((bf16[1024,250]{1,0:T(8,128)(2,1)S(1)}, bf16[1024,250]{1,0:T(8,128)(2,1)S(1)}, u32[]{:S(2)}, u32[]{:S(2)}) %collective-permute-start.2) | collective-permute-done | bytes 512032 | tf_op jit(solution)/shard_map/ppermute | solution.py:20
  109.5 2.5 collective-permute-done.3
  111.9 0.3 pad_maximum_fusion.1
  112.3 10.4 %gather_fusion.1 = bf16[272,128,250]{2,1,0:T(8,128)(2,1)} fusion(bf16[32,128,250]{2,1,0:T(8,128)(2,1)S(1)} %bitcast.98, s32[1024]{0:T(1024)S(1)} %pad_clamp_fusion), kind=kCustom, calls=%fused_computation.1 | custom fusion | bytes 34817088 | tf_op jit(solution)/shard_map/gather | solution.py:58
  122.7 13.6 %multiply_reduce_fusion.2 = (f32[250]{0:T(256)S(1)}, f32[16,250,128]{1,2,0:T(8,128)}) fusion(s32[250]{0:T(256)S(1)} %iota_add_fusion, s32[16,128]{1,0:T(8,128)S(1)} %bitcast.104, f32[250]{0:T(256)S(1)} %copy-done.6, f32[16,128]{1,0:T(8,128)S(1)} %bitcast.110, f32[250]{0:T(256)S(1)} %div.24, f32[16,250,128]{1,2,0:T(8,128)} %copy-done, f32[250]{0:T(256)S(1)} %div.23, ...), kind=kOutput, calls=%fused_computation.40 | convolution fusion | flops 2244095744 | bytes 30438552 | tf_op jit(solution)/shard_map/rkij,rkjc->ric/dot_general | solution.py:60
  136.3 21.1 %psum.52 = f32[250]{0:T(256)S(1)} all-reduce(f32[250]{0:T(256)S(1)} %get-tuple-element.16), channel_id=1, replica_groups=mesh['rows'=8,'cols'=4] {'rows'}, use_global_device_ids=true, to_apply=%region_7.8 | all-reduce | flops 250 | bytes 2000 | tf_op jit(solution)/shard_map/psum | solution.py:64
  157.5 2.5 multiply_reduce_fusion.1
  159.9 19.0 %psum.53 = f32[250]{0:T(256)S(1)} all-reduce(f32[250]{0:T(256)S(1)} %multiply_reduce_fusion.1), channel_id=1, replica_groups=mesh['rows'=8,'cols'=4] {'rows'}, use_global_device_ids=true, to_apply=%region_9.10 | all-reduce | flops 250 | bytes 2000 | tf_op jit(solution)/shard_map/psum | solution.py:49
  178.9 2.5 fusion.26
  181.4 0.1 fusion.32
  181.5 2.3 collective-permute-start.4
  183.8 2.4 collective-permute-start.5
  186.3 9.9 %collective-permute-done.4 = bf16[1024,250]{1,0:T(8,128)(2,1)S(1)} collective-permute-done((bf16[1024,250]{1,0:T(8,128)(2,1)S(1)}, bf16[1024,250]{1,0:T(8,128)(2,1)S(1)}, u32[]{:S(2)}, u32[]{:S(2)}) %collective-permute-start.4) | collective-permute-done | bytes 512032 | tf_op jit(solution)/shard_map/ppermute | solution.py:20
  196.1 2.5 collective-permute-done.5
  198.6 0.3 pad_maximum_fusion.2
  199.0 10.4 %gather_fusion.2 = bf16[272,128,250]{2,1,0:T(8,128)(2,1)} fusion(bf16[32,128,250]{2,1,0:T(8,128)(2,1)S(1)} %bitcast.96, s32[1024]{0:T(1024)S(1)} %pad_clamp_fusion), kind=kCustom, calls=%fused_computation.2 | custom fusion | bytes 34817088 | tf_op jit(solution)/shard_map/gather | solution.py:58
  209.4 14.8 %fusion.12 = (f32[250]{0:T(256)S(1)}, f32[16,250,128]{1,2,0:T(8,128)}) fusion(f32[250]{0:T(256)S(1)} %div.26, s32[250]{0:T(256)S(1)} %iota_add_fusion, s32[16,128]{1,0:T(8,128)S(1)} %bitcast.106, f32[250]{0:T(256)S(1)} %copy-done.6, f32[16,128]{1,0:T(8,128)S(1)} %bitcast.112, f32[250]{0:T(256)S(1)} %div.24, f32[16,250,128]{1,2,0:T(8,128)} %get-tuple-element.17, ...), kind=kOutput, calls=%fused_computation.16 | convolution fusion | flops 2246655744 | bytes 32488552 | tf_op jit(solution)/shard_map/rkij,rkjc->ric/dot_general | solution.py:60
  224.2 17.1 %psum.54 = f32[250]{0:T(256)S(1)} all-reduce(f32[250]{0:T(256)S(1)} %get-tuple-element.18), channel_id=1, replica_groups=mesh['rows'=8,'cols'=4] {'rows'}, use_global_device_ids=true, to_apply=%region_11.12 | all-reduce | flops 250 | bytes 2000 | tf_op jit(solution)/shard_map/psum | solution.py:64
  241.3 3.1 %multiply_reduce_fusion = f32[16,128]{1,0:T(8,128)S(1)} fusion(f32[250]{0:T(256)S(1)} %div.27, f32[250]{0:T(256)S(1)} %div.26, f32[250]{0:T(256)S(1)} %div.25, f32[250]{0:T(256)S(1)} %div.23, s32[250]{0:T(256)S(1)} %iota_add_fusion, s32[16,128]{1,0:T(8,128)S(1)} %bitcast.107, f32[250]{0:T(256)S(1)} %copy-done.6, f32[16,128]{1,0:T(8,128)S(1)} %bitcast.113, ...), kind=kLoop, calls=%fused_computation.34 | loop fusion | flops 11261952 | bytes 4127576 | tf_op jit(solution)/shard_map/reduce_sum | solution.py:71
  244.4 5.8 %psum.55 = f32[2048]{0:T(1024)S(1)} all-reduce(f32[2048]{0:T(1024)S(1)} %bitcast.114), channel_id=1, replica_groups=mesh['rows'=8,'cols'=4] {'cols'}, use_global_device_ids=true, to_apply=%region_13.14 | all-reduce | flops 2048 | bytes 16384 | tf_op jit(solution)/shard_map/psum | solution.py:71
  250.2 6.1 %fusion.14 = (f32[2048,250]{1,0:T(8,128)}, f32[2048,250]{1,0:T(8,128)}) fusion(f32[16,250,128]{1,2,0:T(8,128)} %get-tuple-element.19, f32[250]{0:T(256)S(1)} %div.27, f32[250]{0:T(256)S(1)} %div.26, f32[16,250,128]{1,2,0:T(8,128)} %get-tuple-element.17, f32[250]{0:T(256)S(1)} %div.25, f32[16,250,128]{1,2,0:T(8,128)S(1)} %copy-done.2, f32[250]{0:T(256)S(1)} %div.23, ...), kind=kLoop, calls=%fused_computation.22 | loop fusion | flops 12288000 | bytes 10271576 | tf_op jit(solution)/shard_map/sub | solution.py:67
  (18 shorter events, 0.1 us)
Async XLA Ops:
  0.6 7.7 %copy-start.7 = (s32[16,17]{1,0:T(8,128)S(1)}, s32[16,17]{1,0:T(8,128)}, u32[]{:S(2)}) copy-start(s32[16,17]{1,0:T(8,128)} %param.7) | copy-start | bytes 3268
  0.6 7.8 %copy-start.8 = (s32[16]{0:T(128)S(1)}, s32[16]{0:T(128)}, u32[]{:S(2)}) copy-start(s32[16]{0:T(128)} %param.8) | copy-start | bytes 196
  2.2 25.4 %collective-permute-start = (bf16[1024,250]{1,0:T(8,128)(2,1)S(1)}, bf16[1024,250]{1,0:T(8,128)(2,1)S(1)}, u32[]{:S(2)}, u32[]{:S(2)}) collective-permute-start(bf16[1024,250]{1,0:T(8,128)(2,1)S(1)} %get-tuple-element.10), channel_id=1, source_target_pairs={{0,4},{4,8},{8,12},{12,16},{16,20},{20,24},{24,28},{28,0},{1,5},{5... | collective-permute-start | bytes 1536008 | tf_op jit(solution)/shard_map/ppermute | solution.py:20
  5.2 24.7 %collective-permute-start.1 = (bf16[1024,250]{1,0:T(8,128)(2,1)S(1)}, bf16[1024,250]{1,0:T(8,128)(2,1)}, u32[]{:S(2)}, u32[]{:S(2)}) collective-permute-start(bf16[1024,250]{1,0:T(8,128)(2,1)S(1)} %get-tuple-element.11), channel_id=1, source_target_pairs={{4,0},{8,4},{12,8},{16,12},{20,16},{24,20},{28,24},{0,28},{5,1},{9... | collective-permute-start | bytes 1536008 | tf_op jit(solution)/shard_map/ppermute | solution.py:22
  27.6 0.8 copy-start.3
  31.5 10.5 %copy-start.4 = (s32[2048]{0:T(1024)S(1)}, s32[2048]{0:T(1024)}, u32[]{:S(2)}) copy-start(s32[2048]{0:T(1024)} %param.9) | copy-start | bytes 24580
  31.5 10.4 %copy-start.5 = (f32[2048]{0:T(1024)S(1)}, f32[2048]{0:T(1024)}, u32[]{:S(2)}) copy-start(f32[2048]{0:T(1024)} %param.10) | copy-start | bytes 24580
  31.5 10.4 %copy-start.6 = (f32[250]{0:T(256)S(1)}, f32[250]{0:T(256)}, u32[]{:S(2)}) copy-start(f32[250]{0:T(256)} %param.11) | copy-start | bytes 3004
  52.3 40.5 %copy-start = (f32[16,250,128]{1,2,0:T(8,128)}, f32[16,250,128]{1,2,0:T(8,128)S(1)}, u32[]{:S(2)}) copy-start(f32[16,250,128]{1,2,0:T(8,128)S(1)} %get-tuple-element.15) | copy-start | bytes 6144004
  93.0 16.5 %collective-permute-start.2 = (bf16[1024,250]{1,0:T(8,128)(2,1)S(1)}, bf16[1024,250]{1,0:T(8,128)(2,1)S(1)}, u32[]{:S(2)}, u32[]{:S(2)}) collective-permute-start(bf16[1024,250]{1,0:T(8,128)(2,1)S(1)} %get-tuple-element.8), channel_id=1, source_target_pairs={{0,4},{4,8},{8,12},{12,16},{16,20},{20,24},{24,28},{28,0},{1,5},{5... | collective-permute-start | bytes 1536008 | tf_op jit(solution)/shard_map/ppermute | solution.py:20
  97.1 14.8 %collective-permute-start.3 = (bf16[1024,250]{1,0:T(8,128)(2,1)S(1)}, bf16[1024,250]{1,0:T(8,128)(2,1)S(1)}, u32[]{:S(2)}, u32[]{:S(2)}) collective-permute-start(bf16[1024,250]{1,0:T(8,128)(2,1)S(1)} %get-tuple-element.9), channel_id=1, source_target_pairs={{4,0},{8,4},{12,8},{16,12},{20,16},{24,20},{28,24},{0,28},{5,1},{9... | collective-permute-start | bytes 1536008 | tf_op jit(solution)/shard_map/ppermute | solution.py:22
  122.7 34.8 %copy-start.1 = (f32[16,250,128]{1,2,0:T(8,128)S(1)}, f32[16,250,128]{1,2,0:T(8,128)}, u32[]{:S(2)}) copy-start(f32[16,250,128]{1,2,0:T(8,128)} %copy-done) | copy-start | bytes 6144004
  181.5 14.6 %collective-permute-start.4 = (bf16[1024,250]{1,0:T(8,128)(2,1)S(1)}, bf16[1024,250]{1,0:T(8,128)(2,1)S(1)}, u32[]{:S(2)}, u32[]{:S(2)}) collective-permute-start(bf16[1024,250]{1,0:T(8,128)(2,1)S(1)} %get-tuple-element.6), channel_id=1, source_target_pairs={{0,4},{4,8},{8,12},{12,16},{16,20},{20,24},{24,28},{28,0},{1,5},{5... | collective-permute-start | bytes 1536008 | tf_op jit(solution)/shard_map/ppermute | solution.py:20
  183.8 14.8 %collective-permute-start.5 = (bf16[1024,250]{1,0:T(8,128)(2,1)S(1)}, bf16[1024,250]{1,0:T(8,128)(2,1)S(1)}, u32[]{:S(2)}, u32[]{:S(2)}) collective-permute-start(bf16[1024,250]{1,0:T(8,128)(2,1)S(1)} %get-tuple-element.7), channel_id=1, source_target_pairs={{4,0},{8,4},{12,8},{16,12},{20,16},{24,20},{28,24},{0,28},{5,1},{9... | collective-permute-start | bytes 1536008 | tf_op jit(solution)/shard_map/ppermute | solution.py:22
  209.4 31.9 %copy-start.2 = (f32[16,250,128]{1,2,0:T(8,128)S(1)}, f32[16,250,128]{1,2,0:T(8,128)}, u32[]{:S(2)}) copy-start(f32[16,250,128]{1,2,0:T(8,128)} %copy-done) | copy-start | bytes 6144004
where the time goes:
time: 257 us; the launch traced here: 256 us
  blocking collectives  102 us (40%)
  waiting for transfers between devices  43.7 us (17%)
  matrix products  38.8 us (15%)
  local copies, waits for them, and re-layouts  32.4 us (13%)
  other arithmetic  20 us (8%)
  starting transfers between devices  19.2 us (7%)
    psum x3, blocking collectives, squares(): return lax.psum(jnp.sum(residual * residual, axis=0), 'rows')  57.5 us
    dot_general x3, matrix products, body(): jnp.einsum('rkij,rkjc->ric', graph_tiles, picked, preferred_element_type=...  38.8 us
    psum x2, blocking collectives, body(): curve_sum = lax.psum(jnp.sum(direction * applied, axis=0), 'rows')  38.3 us
    ppermute x3, waiting for transfers between devices, padded(): lax.ppermute(tail, axis, [(i, (i + 1) % count) for i in range(count)])  37.2 us
    gather x3, local copies, waits for them, and re-layouts, body(): picked = blocks[local_col]  31.2 us
    ppermute x3, starting transfers between devices, padded(): lax.ppermute(head, axis, [((i + 1) % count, i) for i in range(count)])  9.67 us
    ppermute x3, starting transfers between devices, padded(): lax.ppermute(tail, axis, [(i, (i + 1) % count) for i in range(count)])  9.5 us
    ppermute x3, waiting for transfers between devices, padded(): lax.ppermute(head, axis, [((i + 1) % count, i) for i in range(count)])  6.48 us
  transfers between devices with their start and end apart: 6, of which 6 were waited for; matrix products, arithmetic and copies ran while one was open for 0% of the time, Pallas kernels for 0%

commit v1 on v0

v1 whole, which is shorter than its diff:
```python
import functools
import jax
import jax.numpy as jnp
from jax import lax
from jax.experimental import pallas as pl
from jax.experimental.pallas import tpu as pltpu
from jax.sharding import PartitionSpec as P

ITERS = 3


damping = 0.99
smoothing = 0.1


def edges(cells, width):
    count = lax.axis_size("rows")
    ahead = [(i, (i + 1) % count) for i in range(count)]
    behind = [((i + 1) % count, i) for i in range(count)]
    left = lax.ppermute(cells[-width:], "rows", ahead)
    right = lax.ppermute(cells[:width], "rows", behind)
    return jnp.concatenate([left, cells, right], axis=0)


def product_kernel(index_ref, count_ref, tiles_ref, blocks_ref, direction_ref, residual_ref, image_ref, dots_ref):
    row = pl.program_id(0)
    slots = tiles_ref.shape[1]
    live = count_ref[row]
    lhs = jnp.concatenate([tiles_ref[0, k] for k in range(slots)], axis=1)
    picked = []
    for k in range(slots):
        block = blocks_ref[index_ref[row, k]]
        picked.append(jnp.where(k < live, block, jnp.zeros_like(block)))
    rhs = jnp.concatenate(picked, axis=0)
    total = jnp.dot(lhs, rhs, preferred_element_type=jnp.float32)
    direction = direction_ref[0]
    residual = residual_ref[0]
    image = direction - damping * total
    image_ref[0] = image

    @pl.when(row == 0)
    def _():
        dots_ref[...] = jnp.zeros_like(dots_ref)

    def add(at, value):
        dots_ref[at : at + 1] += jnp.sum(value, axis=0, keepdims=True)

    add(0, direction * image)
    add(1, residual * image)
    add(2, image * image)
    add(3, residual * residual)


def product(index, count, tiles, blocks, direction, residual):
    rows, slots, size, _ = tiles.shape
    span, _, classes = blocks.shape
    by_row = pl.BlockSpec((1, size, classes), lambda i, a, b: (i, 0, 0))
    return pl.pallas_call(
        product_kernel,
        grid_spec=pltpu.PrefetchScalarGridSpec(
            num_scalar_prefetch=2,
            grid=(rows,),
            in_specs=[
                pl.BlockSpec((1, slots, size, size), lambda i, a, b: (i, 0, 0, 0)),
                pl.BlockSpec((span, size, classes), lambda i, a, b: (0, 0, 0)),
                by_row,
                by_row,
            ],
            out_specs=[by_row, pl.BlockSpec((8, classes), lambda i, a, b: (0, 0))],
        ),
        out_shape=[
            jax.ShapeDtypeStruct((rows, size, classes), jnp.float32),
            jax.ShapeDtypeStruct((8, classes), jnp.float32),
        ],
        compiler_params=pltpu.CompilerParams(vmem_limit_bytes=32 * 2**20),
    )(index, count, tiles, blocks, direction, residual)


def body(graph_tiles, tile_column, tile_count, class_label, confidence, class_weight):
    block_rows, slot_count, block_size, _ = graph_tiles.shape
    class_dev = class_weight.shape[0]
    half_span = block_rows // 2
    total_blocks = block_rows * lax.axis_size("rows")
    first_row = lax.axis_index("rows") * block_rows - half_span
    index = jnp.mod(tile_column - first_row, total_blocks)
    index = jnp.minimum(index, block_rows + 2 * half_span - 1)
    class_ids = lax.axis_index("cols") * class_dev + jnp.arange(class_dev, dtype=jnp.int32)
    width = half_span * block_size
    labels = edges(class_label, width).reshape(-1, block_size, 1)
    weights = edges(confidence, width).reshape(-1, block_size, 1)
    onehot = (labels == class_ids).astype(jnp.float32)
    prior = (
        weights
        * class_weight
        * ((1.0 - smoothing) * onehot + smoothing / (class_dev * lax.axis_size("cols")))
    )
    residual = direction = prior[half_span:-half_span]
    half = prior.astype(jnp.bfloat16)
    solved = 0.0
    for step in range(ITERS):
        if step:
            half = edges(direction.astype(jnp.bfloat16), half_span)
        image, dots = product(index, tile_count, graph_tiles, half, direction, residual)
        dots = lax.psum(dots, "rows")
        if step == 0:
            norm_now = dots[3]
        step_size = norm_now / dots[0]
        solved = solved + step_size * direction
        residual = residual - step_size * image
        if step < ITERS - 1:
            norm_next = norm_now + step_size * (step_size * dots[2] - 2.0 * dots[1])
            norm_next = jnp.maximum(norm_next, 0.0)
            direction = residual + (norm_next / norm_now) * direction
            norm_now = norm_next
    row_squares = lax.psum(jnp.sum(solved * solved, axis=2), "cols")
    length = jnp.sqrt(row_squares + 1e-06)
    flat = (block_rows * block_size, class_dev)
    return ((solved / length[:, :, None]).reshape(flat), residual.reshape(flat))


def solution(mesh):
    placed = (
        P("rows", None, None, None),
        P("rows", None),
        P("rows"),
        P("rows"),
        P("rows"),
        P("cols"),
    )
    return jax.shard_map(
        body,
        mesh=mesh,
        in_specs=placed,
        out_specs=(P("rows", "cols"), P("rows", "cols")),
        check_vma=False,
    )
```

time: 257 us -> 174 us (0.68)
  matrix products: 38.8 us -> 0 us
  blocking collectives: 102 us -> 64.6 us
  Pallas kernels: 0 us -> 21.9 us
  local copies, waits for them, and re-layouts: 32.4 us -> 15.2 us
  waiting for transfers between devices: 43.7 us -> 30.5 us
    dot_general x3 -> x0, matrix products: 38.8 us -> none  [body(): jnp.einsum('rkij,rkjc->ric', graph_tiles, picked, preferred_element_type=...]
    psum x6 -> x4, blocking collectives: 102 us -> 64.6 us  [the longest x3 58.9 us: body(): dots = lax.psum(dots, 'rows')]
    gather x3 -> x0, local copies, waits for them, and re-layouts: 31.2 us -> none  [body(): picked = blocks[local_col]]
    pallas_call x0 -> x3, Pallas kernels: none -> 21.9 us  [product(): pl.pallas_call(product_kernel, grid_spec=pltpu.PrefetchScalarGridSpec(num...]
    ppermute x6 -> x8, waiting for transfers between devices: 43.7 us -> 30.5 us  [the longest x4 26.1 us: edges(): left = lax.ppermute(cells[-width:], 'rows', ahead)]
    unnamed x18 -> x22, local copies, waits for them, and re-layouts: 0.83 us -> 13.5 us
    sub x1 -> x0, other arithmetic: 6.11 us -> none  [body(): residual = residual - step_size[None, :] * applied]
    convert_element_type x2 -> x3, other arithmetic: 3.52 us -> 7.75 us  [the longest x2 5.68 us: body(): half = edges(direction.astype(jnp.bfloat16), half_span)]
  transfers between devices with their start and end apart: 6 -> 8, of which waited for: 6 -> 5; matrix products, arithmetic and copies ran while one was open for 0% -> 1% of each run, Pallas kernels for 0% -> 0%
where the time goes in v1:
time: 174 us; the launch traced here: 173 us
  blocking collectives  64.6 us (37%)
  waiting for transfers between devices  30.5 us (18%)
  Pallas kernels  21.9 us (13%)
  starting transfers between devices  20.2 us (12%)
  other arithmetic  20 us (11%)
  local copies, waits for them, and re-layouts  15.2 us (9%)
    psum x3, blocking collectives, body(): dots = lax.psum(dots, 'rows')  58.9 us
    ppermute x4, waiting for transfers between devices, edges(): left = lax.ppermute(cells[-width:], 'rows', ahead)  26.1 us
    pallas_call x3, Pallas kernels, product(): pl.pallas_call(product_kernel, grid_spec=pltpu.PrefetchScalarGridSpec(num...  21.9 us
    ppermute x4, starting transfers between devices, edges(): right = lax.ppermute(cells[:width], 'rows', behind)  15.8 us
    unnamed x22, local copies, waits for them, and re-layouts  13.5 us
    reduce_sum x1, other arithmetic, body(): row_squares = lax.psum(jnp.sum(solved * solved, axis=2), 'cols')  6.01 us
    psum x1, blocking collectives, body(): row_squares = lax.psum(jnp.sum(solved * solved, axis=2), 'cols')  5.73 us
    convert_element_type x2, other arithmetic, body(): half = edges(direction.astype(jnp.bfloat16), half_span)  5.68 us
  transfers between devices with their start and end apart: 8, of which 5 were waited for; matrix products, arithmetic and copies ran while one was open for 1% of the time, Pallas kernels for 0%

profile of v1, /device:TPU:0, one launch (start us, length us, event | category | flops | bytes accessed | tf_op | source)
XLA Modules:
  0.0 173.4 jit_solution(7257494213002450699)
XLA Ops:
  0.6 0.7 fusion.12
  1.3 2.9 %collective-permute-start = (f32[1024]{0:T(1024)S(1)}, f32[1024]{0:T(1024)S(1)}, u32[]{:S(2)}, u32[]{:S(2)}) collective-permute-start(f32[1024]{0:T(1024)S(1)} %get-tuple-element.40), channel_id=1, source_target_pairs={{0,4},{4,8},{8,12},{12,16},{16,20},{20,24},{24,28},{28,0},{1,5},{5... | collective-permute-start | bytes 12296 | tf_op jit(solution)/shard_map/ppermute | solution.py:20
  4.3 3.0 %collective-permute-start.1 = (f32[1024]{0:T(1024)S(1)}, f32[1024]{0:T(1024)S(1)}, u32[]{:S(2)}, u32[]{:S(2)}) collective-permute-start(f32[1024]{0:T(1024)S(1)} %get-tuple-element.41), channel_id=1, source_target_pairs={{4,0},{8,4},{12,8},{16,12},{20,16},{24,20},{28,24},{0,28},{5,1},{9... | collective-permute-start | bytes 12296 | tf_op jit(solution)/shard_map/ppermute | solution.py:21
  7.3 0.7 fusion.13
  8.0 4.7 %collective-permute-start.3 = (s32[1024]{0:T(1024)S(1)}, s32[1024]{0:T(1024)S(1)}, u32[]{:S(2)}, u32[]{:S(2)}) collective-permute-start(s32[1024]{0:T(1024)S(1)} %get-tuple-element.43), channel_id=1, source_target_pairs={{4,0},{8,4},{12,8},{16,12},{20,16},{24,20},{28,24},{0,28},{5,1},{9... | collective-permute-start | bytes 12296 | tf_op jit(solution)/shard_map/ppermute | solution.py:21
  12.7 0.7 fusion.2.index_ref
  13.5 0.7 maximum_bitcast_fusion
  14.2 0.1 collective-permute-done.2
  14.3 0.7 add_bitcast_fusion
  15.0 2.1 %fusion = (bf16[32,128,250]{2,1,0:T(8,128)(2,1)S(1)}, f32[32,128,250]{2,1,0:T(8,128)S(1)}) fusion(s32[250]{0:T(256)S(1)} %iota_add_fusion, s32[32,128]{1,0:T(8,128)S(1)} %add_bitcast_fusion, f32[250]{0:T(256)} %param.11, f32[32,128]{1,0:T(8,128)S(1)} %maximum_bitcast_fusion), kind=kLoop, calls=%fused_computation.11 | loop fusion | flops 6144000 | bytes 6178768 | tf_op jit(solution)/shard_map/convert_element_type | solution.py:98
  17.1 0.0 copy-start.9
  17.1 0.1 slice.68.direction_ref.residual_ref
  17.3 1.8 %copy-done.10 = f32[32,128,250]{2,1,0:T(8,128)} copy-done((f32[32,128,250]{2,1,0:T(8,128)}, f32[32,128,250]{2,1,0:T(8,128)S(1)}, u32[]{:S(2)}) %copy-start.10) | copy-done | bytes 4096024
  19.1 0.6 copy-done
  19.7 7.3 %shard_map.77 = (f32[16,128,250]{2,1,0:T(8,128)S(1)}, f32[8,250]{1,0:T(8,128)S(1)}) custom-call(s32[16,17]{1,0:T(8,128)S(1)} %fusion.2.index_ref, s32[16]{0:T(128)S(1)} %copy-done.9, bf16[16,17,128,128]{3,2,1,0:T(8,128)(2,1)S(1)} %copy-done, bf16[32,128,250]{2,1,0:T(8,128)(2,1)S(1)} %get-tuple-element.31.blocks_ref, ...), custom_call_target="tpu_custom_call" | custom-call | tf_op jit(solution)/shard_map/pallas_call | solution.py:58
  27.0 0.0 copy-start.6
  27.0 1.3 copy-done.6
  28.3 22.1 %psum.28 = f32[8,250]{1,0:T(8,128)S(1)} all-reduce(f32[8,250]{1,0:T(8,128)S(1)} %get-tuple-element.8), channel_id=1, replica_groups=mesh['rows'=8,'cols'=4] {'rows'}, use_global_device_ids=true, to_apply=%region_0.1 | all-reduce | flops 2000 | bytes 16000 | tf_op jit(solution)/shard_map/psum | solution.py:104
  50.4 2.8 %fusion.6 = (bf16[16,128,250]{2,1,0:T(8,128)(2,1)S(1)}, f32[16,128,250]{2,1,0:T(8,128)S(1)}, f32[16,128,250]{2,1,0:T(8,128)S(1)}) fusion(f32[32,128,250]{2,1,0:T(8,128)} %copy-done.10, f32[250]{0:T(256)S(1)} %get-tuple-element.24, f32[16,128,250]{2,1,0:T(8,128)} %copy-done.6, f32[250]{0:T(256)S(1)} %get-tuple-element.26), kind=kLoop, calls=%fused_computation.28 | loop fusion | flops 2560000 | bytes 9218000 | tf_op jit(solution)/shard_map/convert_element_type | solution.py:102
  53.3 0.0 copy-start.5
  53.3 0.1 fusion.9
  53.4 0.1 collective-permute-start.4
  53.5 4.7 %collective-permute-start.5 = (bf16[8,128,250]{2,1,0:T(8,128)(2,1)S(1)}, bf16[8,128,250]{2,1,0:T(8,128)(2,1)S(1)}, u32[]{:S(2)}, u32[]{:S(2)}) collective-permute-start(bf16[8,128,250]{2,1,0:T(8,128)(2,1)S(1)} %get-tuple-element.30), channel_id=1, source_target_pairs={{4,0},{8,4},{12,8},{16,12},{20,16},{24,20},{28,24},{0,28},{5,1},{9... | collective-permute-start | bytes 1536008 | tf_op jit(solution)/shard_map/ppermute | solution.py:21
  58.2 12.5 %collective-permute-done.4 = bf16[8,128,250]{2,1,0:T(8,128)(2,1)S(1)} collective-permute-done((bf16[8,128,250]{2,1,0:T(8,128)(2,1)S(1)}, bf16[8,128,250]{2,1,0:T(8,128)(2,1)S(1)}, u32[]{:S(2)}, u32[]{:S(2)}) %collective-permute-start.4) | collective-permute-done | bytes 512032 | tf_op jit(solution)/shard_map/ppermute | solution.py:20
  70.7 2.3 %collective-permute-done.5 = bf16[8,128,250]{2,1,0:T(8,128)(2,1)S(1)} collective-permute-done((bf16[8,128,250]{2,1,0:T(8,128)(2,1)S(1)}, bf16[8,128,250]{2,1,0:T(8,128)(2,1)S(1)}, u32[]{:S(2)}, u32[]{:S(2)}) %collective-permute-start.5) | collective-permute-done | bytes 512032 | tf_op jit(solution)/shard_map/ppermute | solution.py:21
  72.9 0.4 pad_maximum_fusion.blocks_ref
  73.4 3.5 %copy-done.1 = bf16[16,17,128,128]{3,2,1,0:T(8,128)(2,1)S(1)} copy-done((bf16[16,17,128,128]{3,2,1,0:T(8,128)(2,1)S(1)}, bf16[16,17,128,128]{3,2,1,0:T(8,128)(2,1)}, u32[]{:S(2)}) %copy-start.1) | copy-done | bytes 8912920
  76.9 7.3 %shard_map.78 = (f32[16,128,250]{2,1,0:T(8,128)S(1)}, f32[8,250]{1,0:T(8,128)S(1)}) custom-call(s32[16,17]{1,0:T(8,128)S(1)} %fusion.2.index_ref, s32[16]{0:T(128)S(1)} %copy-done.9, bf16[16,17,128,128]{3,2,1,0:T(8,128)(2,1)S(1)} %copy-done.1, bf16[32,128,250]{2,1,0:T(8,128)(2,1)S(1)} %pad_maximum_fusion.blocks_ref, ...), custom_call_target="tpu_custom_call" | custom-call | tf_op jit(solution)/shard_map/pallas_call | solution.py:58
  84.2 0.0 copy-start.8
  84.2 1.3 copy-done.8
  85.5 18.0 %psum.29 = f32[8,250]{1,0:T(8,128)S(1)} all-reduce(f32[8,250]{1,0:T(8,128)S(1)} %get-tuple-element.10), channel_id=1, replica_groups=mesh['rows'=8,'cols'=4] {'rows'}, use_global_device_ids=true, to_apply=%region_1.2 | all-reduce | flops 2000 | bytes 16000 | tf_op jit(solution)/shard_map/psum | solution.py:104
  103.5 2.8 %fusion.5 = (bf16[16,128,250]{2,1,0:T(8,128)(2,1)S(1)}, f32[16,128,250]{2,1,0:T(8,128)S(1)}, f32[16,128,250]{2,1,0:T(8,128)S(1)}) fusion(f32[16,128,250]{2,1,0:T(8,128)S(1)} %get-tuple-element.22.direction_ref, f32[250]{0:T(256)S(1)} %get-tuple-element.19, f32[16,128,250]{2,1,0:T(8,128)} %copy-done.5, f32[16,128,250]{2,1,0:T(8,128)} %copy-done.8, ...), kind=kLoop, calls=%fused_computation.27 | loop fusion | flops 2560000 | bytes 11266000 | tf_op jit(solution)/shard_map/convert_element_type | solution.py:102
  106.4 0.0 copy-start.3
  106.4 0.0 copy-start.4
  106.4 0.1 fusion.8
  106.5 1.5 collective-permute-start.6
  108.0 3.3 %collective-permute-start.7 = (bf16[8,128,250]{2,1,0:T(8,128)(2,1)S(1)}, bf16[8,128,250]{2,1,0:T(8,128)(2,1)S(1)}, u32[]{:S(2)}, u32[]{:S(2)}) collective-permute-start(bf16[8,128,250]{2,1,0:T(8,128)(2,1)S(1)} %get-tuple-element.28), channel_id=1, source_target_pairs={{4,0},{8,4},{12,8},{16,12},{20,16},{24,20},{28,24},{0,28},{5,1},{9... | collective-permute-start | bytes 1536008 | tf_op jit(solution)/shard_map/ppermute | solution.py:21
  111.3 13.4 %collective-permute-done.6 = bf16[8,128,250]{2,1,0:T(8,128)(2,1)S(1)} collective-permute-done((bf16[8,128,250]{2,1,0:T(8,128)(2,1)S(1)}, bf16[8,128,250]{2,1,0:T(8,128)(2,1)S(1)}, u32[]{:S(2)}, u32[]{:S(2)}) %collective-permute-start.6) | collective-permute-done | bytes 512032 | tf_op jit(solution)/shard_map/ppermute | solution.py:20
  124.7 2.2 %collective-permute-done.7 = bf16[8,128,250]{2,1,0:T(8,128)(2,1)S(1)} collective-permute-done((bf16[8,128,250]{2,1,0:T(8,128)(2,1)S(1)}, bf16[8,128,250]{2,1,0:T(8,128)(2,1)S(1)}, u32[]{:S(2)}, u32[]{:S(2)}) %collective-permute-start.7) | collective-permute-done | bytes 512032 | tf_op jit(solution)/shard_map/ppermute | solution.py:21
  126.9 0.4 pad_maximum_fusion.1.blocks_ref
  127.3 0.0 copy-start.2
  127.3 3.5 %copy-done.2 = bf16[16,17,128,128]{3,2,1,0:T(8,128)(2,1)S(1)} copy-done((bf16[16,17,128,128]{3,2,1,0:T(8,128)(2,1)S(1)}, bf16[16,17,128,128]{3,2,1,0:T(8,128)(2,1)}, u32[]{:S(2)}) %copy-start.2) | copy-done | bytes 8912920
  130.8 7.3 %shard_map.79 = (f32[16,128,250]{2,1,0:T(8,128)S(1)}, f32[8,250]{1,0:T(8,128)S(1)}) custom-call(s32[16,17]{1,0:T(8,128)S(1)} %fusion.2.index_ref, s32[16]{0:T(128)S(1)} %copy-done.9, bf16[16,17,128,128]{3,2,1,0:T(8,128)(2,1)S(1)} %copy-done.2, bf16[32,128,250]{2,1,0:T(8,128)(2,1)S(1)} %pad_maximum_fusion.1.blocks_ref, ...), custom_call_target="tpu_custom_call" | custom-call | tf_op jit(solution)/shard_map/pallas_call | solution.py:58
  138.2 1.3 copy-done.7
  139.5 18.8 %psum.30 = f32[8,250]{1,0:T(8,128)S(1)} all-reduce(f32[8,250]{1,0:T(8,128)S(1)} %get-tuple-element.12), channel_id=1, replica_groups=mesh['rows'=8,'cols'=4] {'rows'}, use_global_device_ids=true, to_apply=%region_2.3 | all-reduce | flops 2000 | bytes 16000 | tf_op jit(solution)/shard_map/psum | solution.py:104
  158.3 6.0 %multiply_reduce_fusion = (f32[16,128]{1,0:T(8,128)S(1)}, f32[16,128,250]{2,1,0:T(8,128)}, f32[16,128,250]{2,1,0:T(8,128)}) fusion(f32[16,128,250]{2,1,0:T(8,128)} %copy-done.3, f32[250]{0:T(256)S(1)} %fusion.3, f32[16,128,250]{2,1,0:T(8,128)S(1)} %get-tuple-element.22.direction_ref, f32[250]{0:T(256)S(1)} %get-tuple-element.20, ...), kind=kLoop, calls=%fused_computation.4 | loop fusion | flops 4605952 | bytes 14347192 | tf_op jit(solution)/shard_map/reduce_sum | solution.py:115
  164.4 5.7 %psum.31 = f32[16,128]{1,0:T(8,128)S(1)} all-reduce(f32[16,128]{1,0:T(8,128)S(1)} %get-tuple-element.14), channel_id=1, replica_groups=mesh['rows'=8,'cols'=4] {'cols'}, use_global_device_ids=true, to_apply=%region_4.5 | all-reduce | flops 2048 | bytes 16384 | tf_op jit(solution)/shard_map/psum | solution.py:115
  170.1 3.3 %broadcast_divide_fusion = f32[16,128,250]{2,1,0:T(8,128)} fusion(f32[16,128,250]{2,1,0:T(8,128)} %get-tuple-element.15, f32[16,128]{1,0:T(8,128)S(1)} %add_sqrt_fusion), kind=kLoop, calls=%fused_computation.10 | loop fusion | flops 512000 | bytes 4104192 | tf_op jit(solution)/shard_map/div | solution.py:118
  (20 shorter events, 0.1 us)
Async XLA Ops:
  1.3 12.1 %collective-permute-start = (f32[1024]{0:T(1024)S(1)}, f32[1024]{0:T(1024)S(1)}, u32[]{:S(2)}, u32[]{:S(2)}) collective-permute-start(f32[1024]{0:T(1024)S(1)} %get-tuple-element.40), channel_id=1, source_target_pairs={{0,4},{4,8},{8,12},{12,16},{16,20},{20,24},{24,28},{28,0},{1,5},{5... | collective-permute-start | bytes 12296 | tf_op jit(solution)/shard_map/ppermute | solution.py:20
  4.3 9.2 %collective-permute-start.1 = (f32[1024]{0:T(1024)S(1)}, f32[1024]{0:T(1024)S(1)}, u32[]{:S(2)}, u32[]{:S(2)}) collective-permute-start(f32[1024]{0:T(1024)S(1)} %get-tuple-element.41), channel_id=1, source_target_pairs={{4,0},{8,4},{12,8},{16,12},{20,16},{24,20},{28,24},{0,28},{5,1},{9... | collective-permute-start | bytes 12296 | tf_op jit(solution)/shard_map/ppermute | solution.py:21
  8.0 6.3 %collective-permute-start.2 = (s32[1024]{0:T(1024)S(1)}, s32[1024]{0:T(1024)S(1)}, u32[]{:S(2)}, u32[]{:S(2)}) collective-permute-start(s32[1024]{0:T(1024)S(1)} %get-tuple-element.42), channel_id=1, source_target_pairs={{0,4},{4,8},{8,12},{12,16},{16,20},{20,24},{24,28},{28,0},{1,5},{5... | collective-permute-start | bytes 12296 | tf_op jit(solution)/shard_map/ppermute | solution.py:20
  8.0 6.3 %collective-permute-start.3 = (s32[1024]{0:T(1024)S(1)}, s32[1024]{0:T(1024)S(1)}, u32[]{:S(2)}, u32[]{:S(2)}) collective-permute-start(s32[1024]{0:T(1024)S(1)} %get-tuple-element.43), channel_id=1, source_target_pairs={{4,0},{8,4},{12,8},{16,12},{20,16},{24,20},{28,24},{0,28},{5,1},{9... | collective-permute-start | bytes 12296 | tf_op jit(solution)/shard_map/ppermute | solution.py:21
  15.0 4.7 %copy-start = (bf16[16,17,128,128]{3,2,1,0:T(8,128)(2,1)S(1)}, bf16[16,17,128,128]{3,2,1,0:T(8,128)(2,1)}, u32[]{:S(2)}) copy-start(bf16[16,17,128,128]{3,2,1,0:T(8,128)(2,1)} %tiles_ref.5) | copy-start | bytes 26738692
  17.1 2.0 %copy-start.10 = (f32[32,128,250]{2,1,0:T(8,128)}, f32[32,128,250]{2,1,0:T(8,128)S(1)}, u32[]{:S(2)}) copy-start(f32[32,128,250]{2,1,0:T(8,128)S(1)} %get-tuple-element.32) | copy-start | bytes 12288004
  17.1 2.6 %copy-start.9 = (s32[16]{0:T(128)S(1)}, s32[16]{0:T(128)}, u32[]{:S(2)}) copy-start(s32[16]{0:T(128)} %count_ref.5) | copy-start | bytes 196
  27.0 1.3 copy-start.6
  53.3 20.1 %copy-start.5 = (f32[16,128,250]{2,1,0:T(8,128)}, f32[16,128,250]{2,1,0:T(8,128)S(1)}, u32[]{:S(2)}) copy-start(f32[16,128,250]{2,1,0:T(8,128)S(1)} %get-tuple-element.23.residual_ref) | copy-start | bytes 6144004
  53.4 17.3 %collective-permute-start.4 = (bf16[8,128,250]{2,1,0:T(8,128)(2,1)S(1)}, bf16[8,128,250]{2,1,0:T(8,128)(2,1)S(1)}, u32[]{:S(2)}, u32[]{:S(2)}) collective-permute-start(bf16[8,128,250]{2,1,0:T(8,128)(2,1)S(1)} %get-tuple-element.29), channel_id=1, source_target_pairs={{0,4},{4,8},{8,12},{12,16},{16,20},{20,24},{24,28},{28,0},{1,5},{5... | collective-permute-start | bytes 1536008 | tf_op jit(solution)/shard_map/ppermute | solution.py:20
  53.5 19.5 %collective-permute-start.5 = (bf16[8,128,250]{2,1,0:T(8,128)(2,1)S(1)}, bf16[8,128,250]{2,1,0:T(8,128)(2,1)S(1)}, u32[]{:S(2)}, u32[]{:S(2)}) collective-permute-start(bf16[8,128,250]{2,1,0:T(8,128)(2,1)S(1)} %get-tuple-element.30), channel_id=1, source_target_pairs={{4,0},{8,4},{12,8},{16,12},{20,16},{24,20},{28,24},{0,28},{5,1},{9... | collective-permute-start | bytes 1536008 | tf_op jit(solution)/shard_map/ppermute | solution.py:21
  73.3 3.5 %copy-start.1 = (bf16[16,17,128,128]{3,2,1,0:T(8,128)(2,1)S(1)}, bf16[16,17,128,128]{3,2,1,0:T(8,128)(2,1)}, u32[]{:S(2)}) copy-start(bf16[16,17,128,128]{3,2,1,0:T(8,128)(2,1)} %tiles_ref.5) | copy-start | bytes 26738692
  84.2 1.3 copy-start.8
  106.4 20.9 %copy-start.3 = (f32[16,128,250]{2,1,0:T(8,128)}, f32[16,128,250]{2,1,0:T(8,128)S(1)}, u32[]{:S(2)}) copy-start(f32[16,128,250]{2,1,0:T(8,128)S(1)} %get-tuple-element.17.direction_ref) | copy-start | bytes 6144004
  106.4 20.9 %copy-start.4 = (f32[16,128,250]{2,1,0:T(8,128)}, f32[16,128,250]{2,1,0:T(8,128)S(1)}, u32[]{:S(2)}) copy-start(f32[16,128,250]{2,1,0:T(8,128)S(1)} %get-tuple-element.18.residual_ref) | copy-start | bytes 6144004
  106.5 18.2 %collective-permute-start.6 = (bf16[8,128,250]{2,1,0:T(8,128)(2,1)S(1)}, bf16[8,128,250]{2,1,0:T(8,128)(2,1)S(1)}, u32[]{:S(2)}, u32[]{:S(2)}) collective-permute-start(bf16[8,128,250]{2,1,0:T(8,128)(2,1)S(1)} %get-tuple-element.27), channel_id=1, source_target_pairs={{0,4},{4,8},{8,12},{12,16},{16,20},{20,24},{24,28},{28,0},{1,5},{5... | collective-permute-start | bytes 1536008 | tf_op jit(solution)/shard_map/ppermute | solution.py:20
  108.0 18.9 %collective-permute-start.7 = (bf16[8,128,250]{2,1,0:T(8,128)(2,1)S(1)}, bf16[8,128,250]{2,1,0:T(8,128)(2,1)S(1)}, u32[]{:S(2)}, u32[]{:S(2)}) collective-permute-start(bf16[8,128,250]{2,1,0:T(8,128)(2,1)S(1)} %get-tuple-element.28), channel_id=1, source_target_pairs={{4,0},{8,4},{12,8},{16,12},{20,16},{24,20},{28,24},{0,28},{5,1},{9... | collective-permute-start | bytes 1536008 | tf_op jit(solution)/shard_map/ppermute | solution.py:21
  127.3 3.5 %copy-start.2 = (bf16[16,17,128,128]{3,2,1,0:T(8,128)(2,1)S(1)}, bf16[16,17,128,128]{3,2,1,0:T(8,128)(2,1)}, u32[]{:S(2)}) copy-start(bf16[16,17,128,128]{3,2,1,0:T(8,128)(2,1)} %tiles_ref.5) | copy-start | bytes 26738692
  138.2 1.4 copy-start.7

commit v2 on v1

--- a/solution.py
+++ b/solution.py
@@ -42,18 +42,33 @@
     def _():
         dots_ref[...] = jnp.zeros_like(dots_ref)
 
-    def add(at, value):
-        dots_ref[at : at + 1] += jnp.sum(value, axis=0, keepdims=True)
+    classes = image.shape[1]
 
-    add(0, direction * image)
-    add(1, residual * image)
-    add(2, image * image)
-    add(3, residual * residual)
+    def column(value):
+        return jnp.sum(value, axis=0, keepdims=True)
+
+    def held(at):
+        return dots_ref[at : at + 1, 0:classes]
+
+    weight = column(image * image)
+    best = column(residual * image) / jnp.where(weight > 0, weight, 1.0)
+    rest = residual - best * image
+    low = column(rest * rest)
+    mean, mass, least = held(1), held(2), held(4)
+    total_mass = mass + weight
+    share = weight / jnp.where(total_mass > 0, total_mass, 1.0)
+    gap = best - mean
+    dots_ref[0:1, 0:classes] = held(0) + column(direction * image)
+    dots_ref[1:2, 0:classes] = mean + gap * share
+    dots_ref[2:3, 0:classes] = total_mass
+    dots_ref[3:4, 0:classes] = held(3) + column(residual * residual)
+    dots_ref[4:5, 0:classes] = least + low + gap * gap * (mass * share)
 
 
 def product(index, count, tiles, blocks, direction, residual):
     rows, slots, size, _ = tiles.shape
     span, _, classes = blocks.shape
+    lanes = pl.cdiv(classes, 128) * 128
     by_row = pl.BlockSpec((1, size, classes), lambda i, a, b: (i, 0, 0))
     return pl.pallas_call(
         product_kernel,
@@ -66,14 +81,55 @@
                 by_row,
                 by_row,
             ],
-            out_specs=[by_row, pl.BlockSpec((8, classes), lambda i, a, b: (0, 0))],
+            out_specs=[by_row, pl.BlockSpec((8, lanes), lambda i, a, b: (0, 0))],
         ),
         out_shape=[
             jax.ShapeDtypeStruct((rows, size, classes), jnp.float32),
-            jax.ShapeDtypeStruct((8, classes), jnp.float32),
+            jax.ShapeDtypeStruct((8, lanes), jnp.float32),
         ],
         compiler_params=pltpu.CompilerParams(vmem_limit_bytes=32 * 2**20),
     )(index, count, tiles, blocks, direction, residual)
+
+
+def gather_kernel(axis, count, part_ref, all_ref, send_sem, recv_sem):
+    me = lax.axis_index(axis)
+    barrier = pltpu.get_barrier_semaphore()
+    for ahead in range(1, count):
+        peer = lax.rem(me + ahead, count)
+        pl.semaphore_signal(
+            barrier, inc=1, device_id={axis: peer}, device_id_type=pl.DeviceIdType.MESH
+        )
+    pl.semaphore_wait(barrier, count - 1)
+    copies = []
+    for ahead in range(1, count):
+        peer = lax.rem(me + ahead, count)
+        copy = pltpu.make_async_remote_copy(
+            src_ref=part_ref,
+            dst_ref=all_ref.at[me],
+            send_sem=send_sem.at[ahead],
+            recv_sem=recv_sem.at[ahead],
+            device_id={axis: peer},
+            device_id_type=pl.DeviceIdType.MESH,
+        )
+        copy.start()
+        copies.append(copy)
+    all_ref[me] = part_ref[...]
+    for copy in copies:
+        copy.wait()
+
+
+def gathered(part, axis, collective_id):
+    count = lax.axis_size(axis)
+    return pl.pallas_call(
+        functools.partial(gather_kernel, axis, count),
+        out_shape=jax.ShapeDtypeStruct((count,) + part.shape, part.dtype),
+        in_specs=[pl.BlockSpec(memory_space=pltpu.VMEM)],
+        out_specs=pl.BlockSpec(memory_space=pltpu.VMEM),
+        scratch_shapes=[pltpu.SemaphoreType.DMA((count,)), pltpu.SemaphoreType.DMA((count,))],
+        compiler_params=pltpu.CompilerParams(
+            collective_id=collective_id, has_side_effects=True
+        ),
+    )(part)
 
 
 def body(graph_tiles, tile_column, tile_count, class_label, confidence, class_weight):
@@ -101,18 +157,19 @@
         if step:
             half = edges(direction.astype(jnp.bfloat16), half_span)
         image, dots = product(index, tile_count, graph_tiles, half, direction, residual)
-        dots = lax.psum(dots, "rows")
+        parts = gathered(dots, "rows", 0)[:, :, :class_dev]
+        curve_sum = jnp.sum(parts[:, 0], axis=0)
         if step == 0:
-            norm_now = dots[3]
-        step_size = norm_now / dots[0]
+            norm_now = jnp.sum(parts[:, 3], axis=0)
+        step_size = norm_now / curve_sum
         solved = solved + step_size * direction
         residual = residual - step_size * image
         if step < ITERS - 1:
-            norm_next = norm_now + step_size * (step_size * dots[2] - 2.0 * dots[1])
-            norm_next = jnp.maximum(norm_next, 0.0)
+            aside = parts[:, 1] - step_size
+            norm_next = jnp.sum(parts[:, 4] + aside * aside * parts[:, 2], axis=0)
             direction = residual + (norm_next / norm_now) * direction
             norm_now = norm_next
-    row_squares = lax.psum(jnp.sum(solved * solved, axis=2), "cols")
+    row_squares = jnp.sum(gathered(jnp.sum(solved * solved, axis=2), "cols", 1), axis=0)
     length = jnp.sqrt(row_squares + 1e-06)
     flat = (block_rows * block_size, class_dev)
     return ((solved / length[:, :, None]).reshape(flat), residual.reshape(flat))

time: 174 us -> 155 us (0.89)
  blocking collectives: 64.6 us -> 0 us
  Pallas kernels: 21.9 us -> 52.8 us
  waiting for transfers between devices: 30.5 us -> 38.5 us
  other arithmetic: 20 us -> 24.3 us
  local copies, waits for them, and re-layouts: 15.2 us -> 17 us
    psum x4 -> x0, blocking collectives: 64.6 us -> none  [the longest x3 58.9 us: body(): dots = lax.psum(dots, 'rows')]
    pallas_call x0 -> x4, Pallas kernels: none -> 29.7 us  [gathered(): pl.pallas_call(functools.partial(gather_kernel, axis, count), out_shape=j...]
    ppermute x4, waiting for transfers between devices: 26.1 us -> 34 us  [edges(): left = lax.ppermute(cells[-width:], 'rows', ahead)]
    reduce_sum x1 -> x7, other arithmetic: 6.01 us -> 10.4 us  [the longest x1 6.59 us: body(): jnp.sum(solved * solved, axis=2)]
    unnamed x22 -> x28, local copies, waits for them, and re-layouts: 13.5 us -> 15.2 us
where the time goes in v2:
time: 155 us; the launch traced here: 154 us
  Pallas kernels  52.8 us (34%)
  waiting for transfers between devices  38.5 us (25%)
  other arithmetic  24.3 us (16%)
  starting transfers between devices  20.3 us (13%)
  local copies, waits for them, and re-layouts  17 us (11%)
    ppermute x4, waiting for transfers between devices, edges(): left = lax.ppermute(cells[-width:], 'rows', ahead)  34 us
    pallas_call x4, Pallas kernels, gathered(): pl.pallas_call(functools.partial(gather_kernel, axis, count), out_shape=j...  29.7 us
    pallas_call x3, Pallas kernels, product(): pl.pallas_call(product_kernel, grid_spec=pltpu.PrefetchScalarGridSpec(num...  23.1 us
    unnamed x28, local copies, waits for them, and re-layouts  15.2 us
    ppermute x4, starting transfers between devices, edges(): right = lax.ppermute(cells[:width], 'rows', behind)  15 us
    reduce_sum x1, other arithmetic, body(): jnp.sum(solved * solved, axis=2)  6.59 us
    convert_element_type x2, other arithmetic, body(): half = edges(direction.astype(jnp.bfloat16), half_span)  5.67 us
    ppermute x4, starting transfers between devices, edges(): left = lax.ppermute(cells[-width:], 'rows', ahead)  5.27 us
  transfers between devices with their start and end apart: 8, of which 5 were waited for; matrix products, arithmetic and copies ran while one was open for 1% of the time, Pallas kernels for 0%

profile of v2, /device:TPU:0, one launch (start us, length us, event | category | flops | bytes accessed | tf_op | source)
XLA Modules:
  0.0 153.7 jit_solution(16705744994124973011)
XLA Ops:
  0.6 0.7 fusion.17
  1.3 2.9 %collective-permute-start = (f32[1024]{0:T(1024)S(1)}, f32[1024]{0:T(1024)S(1)}, u32[]{:S(2)}, u32[]{:S(2)}) collective-permute-start(f32[1024]{0:T(1024)S(1)} %get-tuple-element.37), channel_id=1, source_target_pairs={{0,4},{4,8},{8,12},{12,16},{16,20},{20,24},{24,28},{28,0},{1,5},{5... | collective-permute-start | bytes 12296 | tf_op jit(solution)/shard_map/ppermute | solution.py:20
  4.3 3.0 %collective-permute-start.1 = (f32[1024]{0:T(1024)S(1)}, f32[1024]{0:T(1024)S(1)}, u32[]{:S(2)}, u32[]{:S(2)}) collective-permute-start(f32[1024]{0:T(1024)S(1)} %get-tuple-element.38), channel_id=1, source_target_pairs={{4,0},{8,4},{12,8},{16,12},{20,16},{24,20},{28,24},{0,28},{5,1},{9... | collective-permute-start | bytes 12296 | tf_op jit(solution)/shard_map/ppermute | solution.py:21
  7.3 0.7 fusion.18
  8.0 4.7 %collective-permute-start.3 = (s32[1024]{0:T(1024)S(1)}, s32[1024]{0:T(1024)S(1)}, u32[]{:S(2)}, u32[]{:S(2)}) collective-permute-start(s32[1024]{0:T(1024)S(1)} %get-tuple-element.40), channel_id=1, source_target_pairs={{4,0},{8,4},{12,8},{16,12},{20,16},{24,20},{28,24},{0,28},{5,1},{9... | collective-permute-start | bytes 12296 | tf_op jit(solution)/shard_map/ppermute | solution.py:21
  12.7 0.7 fusion.2.index_ref
  13.5 0.7 maximum_bitcast_fusion
  14.2 0.1 collective-permute-done.2
  14.3 0.7 add_bitcast_fusion
  15.0 2.1 %fusion = (bf16[32,128,250]{2,1,0:T(8,128)(2,1)S(1)}, f32[32,128,250]{2,1,0:T(8,128)S(1)}) fusion(s32[250]{0:T(256)S(1)} %iota_add_fusion, s32[32,128]{1,0:T(8,128)S(1)} %add_bitcast_fusion, f32[250]{0:T(256)} %param.11, f32[32,128]{1,0:T(8,128)S(1)} %maximum_bitcast_fusion), kind=kLoop, calls=%fused_computation.11 | loop fusion | flops 6144000 | bytes 6178768 | tf_op jit(solution)/shard_map/convert_element_type | solution.py:154
  17.1 0.1 slice.89.direction_ref.residual_ref
  17.3 1.8 %copy-done.13 = f32[32,128,250]{2,1,0:T(8,128)} copy-done((f32[32,128,250]{2,1,0:T(8,128)}, f32[32,128,250]{2,1,0:T(8,128)S(1)}, u32[]{:S(2)}) %copy-start.13) | copy-done | bytes 4096024
  19.1 0.6 copy-done
  19.7 7.7 %shard_map.77 = (f32[16,128,250]{2,1,0:T(8,128)S(1)}, f32[8,256]{1,0:T(8,128)S(1)}) custom-call(s32[16,17]{1,0:T(8,128)S(1)} %fusion.2.index_ref, s32[16]{0:T(128)S(1)} %copy-done.12, bf16[16,17,128,128]{3,2,1,0:T(8,128)(2,1)S(1)} %copy-done, bf16[32,128,250]{2,1,0:T(8,128)(2,1)S(1)} %get-tuple-element.35.blocks_ref, ...), custom_call_target="tpu_custom_call" | custom-call | tf_op jit(solution)/shard_map/pallas_call | solution.py:73
  27.4 1.3 copy-done.6
  28.7 0.6 copy-done.9
  29.3 8.8 %shard_map.78 = f32[8,8,256]{2,1,0:T(8,128)} custom-call(f32[8,256]{1,0:T(8,128)} %copy-done.9), custom_call_target="tpu_custom_call" | custom-call | tf_op jit(solution)/shard_map/pallas_call | solution.py:123
  38.1 1.1 slice_reduce_fusion.2
  39.2 2.8 %fusion.14 = (bf16[16,128,250]{2,1,0:T(8,128)(2,1)S(1)}, f32[16,128,250]{2,1,0:T(8,128)S(1)}, f32[16,128,250]{2,1,0:T(8,128)S(1)}) fusion(f32[32,128,250]{2,1,0:T(8,128)} %copy-done.13, f32[250]{0:T(256)S(1)} %div.52, f32[16,128,250]{2,1,0:T(8,128)} %copy-done.6, f32[250]{0:T(256)S(1)} %div.51), kind=kLoop, calls=%fused_computation.40 | loop fusion | flops 2560000 | bytes 9218000 | tf_op jit(solution)/shard_map/convert_element_type | solution.py:158
  42.1 0.1 fusion.16
  42.2 1.6 %collective-permute-start.4 = (bf16[8,128,250]{2,1,0:T(8,128)(2,1)S(1)}, bf16[8,128,250]{2,1,0:T(8,128)(2,1)S(1)}, u32[]{:S(2)}, u32[]{:S(2)}) collective-permute-start(bf16[8,128,250]{2,1,0:T(8,128)(2,1)S(1)} %get-tuple-element.26), channel_id=1, source_target_pairs={{0,4},{4,8},{8,12},{12,16},{16,20},{20,24},{24,28},{28,0},{1,5},{5... | collective-permute-start | bytes 1536008 | tf_op jit(solution)/shard_map/ppermute | solution.py:20
  43.8 3.2 %collective-permute-start.5 = (bf16[8,128,250]{2,1,0:T(8,128)(2,1)S(1)}, bf16[8,128,250]{2,1,0:T(8,128)(2,1)S(1)}, u32[]{:S(2)}, u32[]{:S(2)}) collective-permute-start(bf16[8,128,250]{2,1,0:T(8,128)(2,1)S(1)} %get-tuple-element.27), channel_id=1, source_target_pairs={{4,0},{8,4},{12,8},{16,12},{20,16},{24,20},{28,24},{0,28},{5,1},{9... | collective-permute-start | bytes 1536008 | tf_op jit(solution)/shard_map/ppermute | solution.py:21
  47.0 16.4 %collective-permute-done.4 = bf16[8,128,250]{2,1,0:T(8,128)(2,1)S(1)} collective-permute-done((bf16[8,128,250]{2,1,0:T(8,128)(2,1)S(1)}, bf16[8,128,250]{2,1,0:T(8,128)(2,1)S(1)}, u32[]{:S(2)}, u32[]{:S(2)}) %collective-permute-start.4) | collective-permute-done | bytes 512032 | tf_op jit(solution)/shard_map/ppermute | solution.py:20
  63.3 2.2 %collective-permute-done.5 = bf16[8,128,250]{2,1,0:T(8,128)(2,1)S(1)} collective-permute-done((bf16[8,128,250]{2,1,0:T(8,128)(2,1)S(1)}, bf16[8,128,250]{2,1,0:T(8,128)(2,1)S(1)}, u32[]{:S(2)}, u32[]{:S(2)}) %collective-permute-start.5) | collective-permute-done | bytes 512032 | tf_op jit(solution)/shard_map/ppermute | solution.py:21
  65.5 0.4 pad_maximum_fusion.blocks_ref
  66.0 3.5 %copy-done.1 = bf16[16,17,128,128]{3,2,1,0:T(8,128)(2,1)S(1)} copy-done((bf16[16,17,128,128]{3,2,1,0:T(8,128)(2,1)S(1)}, bf16[16,17,128,128]{3,2,1,0:T(8,128)(2,1)}, u32[]{:S(2)}) %copy-start.1) | copy-done | bytes 8912920
  69.5 7.7 %shard_map.79 = (f32[16,128,250]{2,1,0:T(8,128)S(1)}, f32[8,256]{1,0:T(8,128)S(1)}) custom-call(s32[16,17]{1,0:T(8,128)S(1)} %fusion.2.index_ref, s32[16]{0:T(128)S(1)} %copy-done.12, bf16[16,17,128,128]{3,2,1,0:T(8,128)(2,1)S(1)} %copy-done.1, bf16[32,128,250]{2,1,0:T(8,128)(2,1)S(1)} %pad_maximum_fusion.blocks_ref, ...), custom_call_target="tpu_custom_call" | custom-call | tf_op jit(solution)/shard_map/pallas_call | solution.py:73
  77.2 1.3 copy-done.8
  78.5 0.6 copy-done.11
  79.1 7.8 %shard_map.80 = f32[8,8,256]{2,1,0:T(8,128)} custom-call(f32[8,256]{1,0:T(8,128)} %copy-done.11), custom_call_target="tpu_custom_call" | custom-call | tf_op jit(solution)/shard_map/pallas_call | solution.py:123
  87.0 1.0 slice_reduce_fusion.1
  88.0 2.8 %fusion.13 = (bf16[16,128,250]{2,1,0:T(8,128)(2,1)S(1)}, f32[16,128,250]{2,1,0:T(8,128)S(1)}, f32[16,128,250]{2,1,0:T(8,128)S(1)}) fusion(f32[16,128,250]{2,1,0:T(8,128)S(1)} %get-tuple-element.22.direction_ref, f32[250]{0:T(256)S(1)} %div.54, f32[16,128,250]{2,1,0:T(8,128)} %copy-done.3, f32[16,128,250]{2,1,0:T(8,128)} %copy-done.8, f32[250]{0:T(256)S(1)} %div.53), kind=kLoop, calls=%fused_computation.39 | loop fusion | flops 2560000 | bytes 11266000 | tf_op jit(solution)/shard_map/convert_element_type | solution.py:158
  90.9 0.1 fusion.15
  91.0 0.7 collective-permute-start.6
  91.7 4.0 %collective-permute-start.7 = (bf16[8,128,250]{2,1,0:T(8,128)(2,1)S(1)}, bf16[8,128,250]{2,1,0:T(8,128)(2,1)S(1)}, u32[]{:S(2)}, u32[]{:S(2)}) collective-permute-start(bf16[8,128,250]{2,1,0:T(8,128)(2,1)S(1)} %get-tuple-element.25), channel_id=1, source_target_pairs={{4,0},{8,4},{12,8},{16,12},{20,16},{24,20},{28,24},{0,28},{5,1},{9... | collective-permute-start | bytes 1536008 | tf_op jit(solution)/shard_map/ppermute | solution.py:21
  95.8 17.5 %collective-permute-done.6 = bf16[8,128,250]{2,1,0:T(8,128)(2,1)S(1)} collective-permute-done((bf16[8,128,250]{2,1,0:T(8,128)(2,1)S(1)}, bf16[8,128,250]{2,1,0:T(8,128)(2,1)S(1)}, u32[]{:S(2)}, u32[]{:S(2)}) %collective-permute-start.6) | collective-permute-done | bytes 512032 | tf_op jit(solution)/shard_map/ppermute | solution.py:20
  113.3 2.3 %collective-permute-done.7 = bf16[8,128,250]{2,1,0:T(8,128)(2,1)S(1)} collective-permute-done((bf16[8,128,250]{2,1,0:T(8,128)(2,1)S(1)}, bf16[8,128,250]{2,1,0:T(8,128)(2,1)S(1)}, u32[]{:S(2)}, u32[]{:S(2)}) %collective-permute-start.7) | collective-permute-done | bytes 512032 | tf_op jit(solution)/shard_map/ppermute | solution.py:21
  115.5 0.4 pad_maximum_fusion.1.blocks_ref
  116.0 3.5 %copy-done.2 = bf16[16,17,128,128]{3,2,1,0:T(8,128)(2,1)S(1)} copy-done((bf16[16,17,128,128]{3,2,1,0:T(8,128)(2,1)S(1)}, bf16[16,17,128,128]{3,2,1,0:T(8,128)(2,1)}, u32[]{:S(2)}) %copy-start.2) | copy-done | bytes 8912920
  119.5 7.7 %shard_map.81 = (f32[16,128,250]{2,1,0:T(8,128)S(1)}, f32[8,256]{1,0:T(8,128)S(1)}) custom-call(s32[16,17]{1,0:T(8,128)S(1)} %fusion.2.index_ref, s32[16]{0:T(128)S(1)} %copy-done.12, bf16[16,17,128,128]{3,2,1,0:T(8,128)(2,1)S(1)} %copy-done.2, bf16[32,128,250]{2,1,0:T(8,128)(2,1)S(1)} %pad_maximum_fusion.1.blocks_ref, ...), custom_call_target="tpu_custom_call" | custom-call | tf_op jit(solution)/shard_map/pallas_call | solution.py:73
  127.2 1.3 copy-done.7
  128.5 0.6 copy-done.10
  129.1 8.1 %shard_map.82 = f32[8,8,256]{2,1,0:T(8,128)} custom-call(f32[8,256]{1,0:T(8,128)} %copy-done.10), custom_call_target="tpu_custom_call" | custom-call | tf_op jit(solution)/shard_map/pallas_call | solution.py:123
  137.2 0.9 slice_reduce_fusion
  138.1 6.6 %multiply_reduce_fusion = (f32[16,128]{1,0:T(8,128)}, f32[16,128,250]{2,1,0:T(8,128)}, f32[16,128,250]{2,1,0:T(8,128)}) fusion(f32[16,128,250]{2,1,0:T(8,128)} %copy-done.4, f32[250]{0:T(256)S(1)} %div.55, f32[16,128,250]{2,1,0:T(8,128)S(1)} %get-tuple-element.22.direction_ref, f32[250]{0:T(256)S(1)} %div.53, f32[32,128,250]{2,1,0:T(8,128)} %copy-done.13, ...), kind=kLoop, calls=%fused_computation.4 | loop fusion | flops 4605952 | bytes 14347192 | tf_op jit(solution)/shard_map/reduce_sum | solution.py:172
  144.7 5.0 %shard_map.83 = f32[4,16,128]{2,1,0:T(8,128)} custom-call(f32[16,128]{1,0:T(8,128)} %get-tuple-element.16.part_ref), custom_call_target="tpu_custom_call" | custom-call | tf_op jit(solution)/shard_map/pallas_call | solution.py:123
  149.7 0.8 reduce_sum.79
  150.5 3.3 %broadcast_divide_fusion = f32[16,128,250]{2,1,0:T(8,128)} fusion(f32[16,128,250]{2,1,0:T(8,128)} %get-tuple-element.17, f32[16,128]{1,0:T(8,128)S(1)} %add_sqrt_fusion), kind=kLoop, calls=%fused_computation.10 | loop fusion | flops 512000 | bytes 4104192 | tf_op jit(solution)/shard_map/div | solution.py:175
  (31 shorter events, 0.2 us)
Async XLA Ops:
  1.3 12.1 %collective-permute-start = (f32[1024]{0:T(1024)S(1)}, f32[1024]{0:T(1024)S(1)}, u32[]{:S(2)}, u32[]{:S(2)}) collective-permute-start(f32[1024]{0:T(1024)S(1)} %get-tuple-element.37), channel_id=1, source_target_pairs={{0,4},{4,8},{8,12},{12,16},{16,20},{20,24},{24,28},{28,0},{1,5},{5... | collective-permute-start | bytes 12296 | tf_op jit(solution)/shard_map/ppermute | solution.py:20
  4.3 9.2 %collective-permute-start.1 = (f32[1024]{0:T(1024)S(1)}, f32[1024]{0:T(1024)S(1)}, u32[]{:S(2)}, u32[]{:S(2)}) collective-permute-start(f32[1024]{0:T(1024)S(1)} %get-tuple-element.38), channel_id=1, source_target_pairs={{4,0},{8,4},{12,8},{16,12},{20,16},{24,20},{28,24},{0,28},{5,1},{9... | collective-permute-start | bytes 12296 | tf_op jit(solution)/shard_map/ppermute | solution.py:21
  8.0 6.3 %collective-permute-start.2 = (s32[1024]{0:T(1024)S(1)}, s32[1024]{0:T(1024)S(1)}, u32[]{:S(2)}, u32[]{:S(2)}) collective-permute-start(s32[1024]{0:T(1024)S(1)} %get-tuple-element.39), channel_id=1, source_target_pairs={{0,4},{4,8},{8,12},{12,16},{16,20},{20,24},{24,28},{28,0},{1,5},{5... | collective-permute-start | bytes 12296 | tf_op jit(solution)/shard_map/ppermute | solution.py:20
  8.0 6.3 %collective-permute-start.3 = (s32[1024]{0:T(1024)S(1)}, s32[1024]{0:T(1024)S(1)}, u32[]{:S(2)}, u32[]{:S(2)}) collective-permute-start(s32[1024]{0:T(1024)S(1)} %get-tuple-element.40), channel_id=1, source_target_pairs={{4,0},{8,4},{12,8},{16,12},{20,16},{24,20},{28,24},{0,28},{5,1},{9... | collective-permute-start | bytes 12296 | tf_op jit(solution)/shard_map/ppermute | solution.py:21
  15.0 4.7 %copy-start = (bf16[16,17,128,128]{3,2,1,0:T(8,128)(2,1)S(1)}, bf16[16,17,128,128]{3,2,1,0:T(8,128)(2,1)}, u32[]{:S(2)}) copy-start(bf16[16,17,128,128]{3,2,1,0:T(8,128)(2,1)} %tiles_ref.5) | copy-start | bytes 26738692
  17.1 2.0 %copy-start.13 = (f32[32,128,250]{2,1,0:T(8,128)}, f32[32,128,250]{2,1,0:T(8,128)S(1)}, u32[]{:S(2)}) copy-start(f32[32,128,250]{2,1,0:T(8,128)S(1)} %get-tuple-element.36) | copy-start | bytes 12288004
  17.1 2.6 %copy-start.12 = (s32[16]{0:T(128)S(1)}, s32[16]{0:T(128)}, u32[]{:S(2)}) copy-start(s32[16]{0:T(128)} %count_ref.5) | copy-start | bytes 196
  27.4 1.3 copy-start.6
  28.7 0.6 copy-start.9
  42.1 23.9 %copy-start.3 = (f32[16,128,250]{2,1,0:T(8,128)}, f32[16,128,250]{2,1,0:T(8,128)S(1)}, u32[]{:S(2)}) copy-start(f32[16,128,250]{2,1,0:T(8,128)S(1)} %get-tuple-element.23.residual_ref) | copy-start | bytes 6144004
  42.2 21.2 %collective-permute-start.4 = (bf16[8,128,250]{2,1,0:T(8,128)(2,1)S(1)}, bf16[8,128,250]{2,1,0:T(8,128)(2,1)S(1)}, u32[]{:S(2)}, u32[]{:S(2)}) collective-permute-start(bf16[8,128,250]{2,1,0:T(8,128)(2,1)S(1)} %get-tuple-element.26), channel_id=1, source_target_pairs={{0,4},{4,8},{8,12},{12,16},{16,20},{20,24},{24,28},{28,0},{1,5},{5... | collective-permute-start | bytes 1536008 | tf_op jit(solution)/shard_map/ppermute | solution.py:20
  43.8 21.8 %collective-permute-start.5 = (bf16[8,128,250]{2,1,0:T(8,128)(2,1)S(1)}, bf16[8,128,250]{2,1,0:T(8,128)(2,1)S(1)}, u32[]{:S(2)}, u32[]{:S(2)}) collective-permute-start(bf16[8,128,250]{2,1,0:T(8,128)(2,1)S(1)} %get-tuple-element.27), channel_id=1, source_target_pairs={{4,0},{8,4},{12,8},{16,12},{20,16},{24,20},{28,24},{0,28},{5,1},{9... | collective-permute-start | bytes 1536008 | tf_op jit(solution)/shard_map/ppermute | solution.py:21
  65.9 3.5 %copy-start.1 = (bf16[16,17,128,128]{3,2,1,0:T(8,128)(2,1)S(1)}, bf16[16,17,128,128]{3,2,1,0:T(8,128)(2,1)}, u32[]{:S(2)}) copy-start(bf16[16,17,128,128]{3,2,1,0:T(8,128)(2,1)} %tiles_ref.5) | copy-start | bytes 26738692
  77.2 1.3 copy-start.8
  78.5 0.6 copy-start.11
  90.9 25.0 %copy-start.4 = (f32[16,128,250]{2,1,0:T(8,128)}, f32[16,128,250]{2,1,0:T(8,128)S(1)}, u32[]{:S(2)}) copy-start(f32[16,128,250]{2,1,0:T(8,128)S(1)} %get-tuple-element.19.direction_ref) | copy-start | bytes 6144004
  90.9 25.0 %copy-start.5 = (f32[16,128,250]{2,1,0:T(8,128)}, f32[16,128,250]{2,1,0:T(8,128)S(1)}, u32[]{:S(2)}) copy-start(f32[16,128,250]{2,1,0:T(8,128)S(1)} %get-tuple-element.20.residual_ref) | copy-start | bytes 6144004
  91.0 22.3 %collective-permute-start.6 = (bf16[8,128,250]{2,1,0:T(8,128)(2,1)S(1)}, bf16[8,128,250]{2,1,0:T(8,128)(2,1)S(1)}, u32[]{:S(2)}, u32[]{:S(2)}) collective-permute-start(bf16[8,128,250]{2,1,0:T(8,128)(2,1)S(1)} %get-tuple-element.24), channel_id=1, source_target_pairs={{0,4},{4,8},{8,12},{12,16},{16,20},{20,24},{24,28},{28,0},{1,5},{5... | collective-permute-start | bytes 1536008 | tf_op jit(solution)/shard_map/ppermute | solution.py:20
  91.7 23.8 %collective-permute-start.7 = (bf16[8,128,250]{2,1,0:T(8,128)(2,1)S(1)}, bf16[8,128,250]{2,1,0:T(8,128)(2,1)S(1)}, u32[]{:S(2)}, u32[]{:S(2)}) collective-permute-start(bf16[8,128,250]{2,1,0:T(8,128)(2,1)S(1)} %get-tuple-element.25), channel_id=1, source_target_pairs={{4,0},{8,4},{12,8},{16,12},{20,16},{24,20},{28,24},{0,28},{5,1},{9... | collective-permute-start | bytes 1536008 | tf_op jit(solution)/shard_map/ppermute | solution.py:21
  115.9 3.5 %copy-start.2 = (bf16[16,17,128,128]{3,2,1,0:T(8,128)(2,1)S(1)}, bf16[16,17,128,128]{3,2,1,0:T(8,128)(2,1)}, u32[]{:S(2)}) copy-start(bf16[16,17,128,128]{3,2,1,0:T(8,128)(2,1)} %tiles_ref.5) | copy-start | bytes 26738692
  127.2 1.3 copy-start.7
  128.5 0.6 copy-start.10

commit v3 on v2

--- a/solution.py
+++ b/solution.py
@@ -13,13 +13,53 @@
 smoothing = 0.1
 
 
-def edges(cells, width):
-    count = lax.axis_size("rows")
-    ahead = [(i, (i + 1) % count) for i in range(count)]
-    behind = [((i + 1) % count, i) for i in range(count)]
-    left = lax.ppermute(cells[-width:], "rows", ahead)
-    right = lax.ppermute(cells[:width], "rows", behind)
-    return jnp.concatenate([left, cells, right], axis=0)
+def edges_kernel(width, count, cells_ref, wide_ref, send_sem, recv_sem):
+    me = lax.axis_index("rows")
+    right = lax.rem(me + 1, count)
+    left = lax.rem(me + count - 1, count)
+    own = cells_ref.shape[0]
+    barrier = pltpu.get_barrier_semaphore()
+    for peer in (left, right):
+        pl.semaphore_signal(
+            barrier, inc=1, device_id={"rows": peer}, device_id_type=pl.DeviceIdType.MESH
+        )
+    pl.semaphore_wait(barrier, 2)
+    copies = []
+    for at, (peer, source, target) in enumerate(
+        ((right, own - width, 0), (left, 0, own + width))
+    ):
+        copy = pltpu.make_async_remote_copy(
+            src_ref=cells_ref.at[pl.ds(source, width)],
+            dst_ref=wide_ref.at[pl.ds(target, width)],
+            send_sem=send_sem.at[at],
+            recv_sem=recv_sem.at[at],
+            device_id={"rows": peer},
+            device_id_type=pl.DeviceIdType.MESH,
+        )
+        copy.start()
+        copies.append(copy)
+
+    @pl.loop(0, own)
+    def _(block):
+        wide_ref[width + block] = cells_ref[block]
+
+    for copy in copies:
+        copy.wait()
+
+
+def edges(cells, width, collective_id):
+    return pl.pallas_call(
+        functools.partial(edges_kernel, width, lax.axis_size("rows")),
+        out_shape=jax.ShapeDtypeStruct(
+            (cells.shape[0] + 2 * width,) + cells.shape[1:], cells.dtype
+        ),
+        in_specs=[pl.BlockSpec(memory_space=pltpu.VMEM)],
+        out_specs=pl.BlockSpec(memory_space=pltpu.VMEM),
+        scratch_shapes=[pltpu.SemaphoreType.DMA((2,)), pltpu.SemaphoreType.DMA((2,))],
+        compiler_params=pltpu.CompilerParams(
+            collective_id=collective_id, has_side_effects=True, vmem_limit_bytes=16 * 2**20
+        ),
+    )(cells)
 
 
 def product_kernel(index_ref, count_ref, tiles_ref, blocks_ref, direction_ref, residual_ref, image_ref, dots_ref):
@@ -141,10 +181,17 @@
     index = jnp.mod(tile_column - first_row, total_blocks)
     index = jnp.minimum(index, block_rows + 2 * half_span - 1)
     class_ids = lax.axis_index("cols") * class_dev + jnp.arange(class_dev, dtype=jnp.int32)
-    width = half_span * block_size
-    labels = edges(class_label, width).reshape(-1, block_size, 1)
-    weights = edges(confidence, width).reshape(-1, block_size, 1)
-    onehot = (labels == class_ids).astype(jnp.float32)
+    given = jnp.stack(
+        [
+            class_label.astype(jnp.float32).reshape(block_rows, block_size),
+            confidence.reshape(block_rows, block_size),
+        ],
+        axis=1,
+    )
+    given = edges(given, half_span, 2)
+    labels = given[:, 0, :, None]
+    weights = given[:, 1, :, None]
+    onehot = (labels == class_ids.astype(jnp.float32)).astype(jnp.float32)
     prior = (
         weights
         * class_weight
@@ -155,7 +202,7 @@
     solved = 0.0
     for step in range(ITERS):
         if step:
-            half = edges(direction.astype(jnp.bfloat16), half_span)
+            half = edges(direction.astype(jnp.bfloat16), half_span, 3)
         image, dots = product(index, tile_count, graph_tiles, half, direction, residual)
         parts = gathered(dots, "rows", 0)[:, :, :class_dev]
         curve_sum = jnp.sum(parts[:, 0], axis=0)

time: 155 us -> 150 us (0.968)
  Pallas kernels: 52.8 us -> 109 us
  waiting for transfers between devices: 38.5 us -> 0 us
  starting transfers between devices: 20.3 us -> 0 us
    pallas_call x0 -> x3, Pallas kernels: none -> 55.6 us  [edges(): pl.pallas_call(functools.partial(edges_kernel, width, lax.axis_size('rows...]
    ppermute x8 -> x0, waiting for transfers between devices: 38.5 us -> none  [the longest x4 34 us: edges(): left = lax.ppermute(cells[-width:], 'rows', ahead)]
    ppermute x8 -> x0, starting transfers between devices: 20.3 us -> none  [the longest x4 15 us: edges(): right = lax.ppermute(cells[:width], 'rows', behind)]
    slice x4 -> x1, local copies, waits for them, and re-layouts: 1.59 us -> 0.03 us  [body(): weights = given[:, 1, :, None]]
    convert_element_type x2 -> x4, other arithmetic: 5.67 us -> 6.57 us  [the longest x2 5.87 us: body(): half = edges(direction.astype(jnp.bfloat16), half_span, 3)]
  transfers between devices with their start and end apart: 8 -> 0, of which waited for: 5 -> 0; matrix products, arithmetic and copies ran while one was open for 1% -> 0% of each run, Pallas kernels for 0% -> 0%
where the time goes in v3:
time: 150 us; the launch traced here: 149 us
  Pallas kernels  109 us (73%)
  other arithmetic  23.8 us (16%)
  local copies, waits for them, and re-layouts  15.6 us (10%)
    pallas_call x3, Pallas kernels, edges(): pl.pallas_call(functools.partial(edges_kernel, width, lax.axis_size('rows...  55.6 us
    pallas_call x4, Pallas kernels, gathered(): pl.pallas_call(functools.partial(gather_kernel, axis, count), out_shape=j...  30.2 us
    pallas_call x3, Pallas kernels, product(): pl.pallas_call(product_kernel, grid_spec=pltpu.PrefetchScalarGridSpec(num...  23.1 us
    unnamed x28, local copies, waits for them, and re-layouts  15.4 us
    reduce_sum x1, other arithmetic, body(): jnp.sum(solved * solved, axis=2)  6.59 us
    convert_element_type x2, other arithmetic, body(): half = edges(direction.astype(jnp.bfloat16), half_span, 3)  5.87 us
    div x1, other arithmetic, body(): return ((solved / length[:, :, None]).reshape(flat), residual.reshape(flat))  3.26 us

profile of v3, /device:TPU:0, one launch (start us, length us, event | category | flops | bytes accessed | tf_op | source)
XLA Modules:
  0.0 149.2 jit_solution(12805412960696890764)
XLA Ops:
  0.6 0.7 fusion.2.index_ref
  1.4 0.7 convert_element_type.20
  2.1 0.7 pad_maximum_fusion.cells_ref
  2.8 8.2 %shard_map.77 = f32[32,2,128]{2,1,0:T(2,128)S(1)} custom-call(f32[16,2,128]{2,1,0:T(2,128)S(1)} %pad_maximum_fusion.cells_ref), custom_call_target="tpu_custom_call" | custom-call | tf_op jit(solution)/shard_map/pallas_call | solution.py:51
  11.0 0.0 copy-start
  11.0 2.1 %fusion = (bf16[32,128,250]{2,1,0:T(8,128)(2,1)S(1)}, f32[32,128,250]{2,1,0:T(8,128)S(1)}) fusion(f32[250]{0:T(256)S(1)} %add_convert_fusion, f32[32,128]{1,0:T(8,128)S(1)} %bitcast.45, f32[250]{0:T(256)} %param.11, f32[32,128]{1,0:T(8,128)S(1)} %bitcast.44), kind=kLoop, calls=%fused_computation.9 | loop fusion | flops 6144000 | bytes 6178768 | tf_op jit(solution)/shard_map/convert_element_type | solution.py:201
  13.1 0.0 copy-start.13
  13.2 1.9 %copy-done.13 = f32[32,128,250]{2,1,0:T(8,128)} copy-done((f32[32,128,250]{2,1,0:T(8,128)}, f32[32,128,250]{2,1,0:T(8,128)S(1)}, u32[]{:S(2)}) %copy-start.13) | copy-done | bytes 4096024
  15.1 0.1 slice.65.direction_ref.residual_ref
  15.2 0.4 copy-done
  15.7 0.2 copy-done.12
  15.9 7.7 %shard_map.78 = (f32[16,128,250]{2,1,0:T(8,128)S(1)}, f32[8,256]{1,0:T(8,128)S(1)}) custom-call(s32[16,17]{1,0:T(8,128)S(1)} %fusion.2.index_ref, s32[16]{0:T(128)S(1)} %copy-done.12, bf16[16,17,128,128]{3,2,1,0:T(8,128)(2,1)S(1)} %copy-done, bf16[32,128,250]{2,1,0:T(8,128)(2,1)S(1)} %get-tuple-element.31.blocks_ref, ...), custom_call_target="tpu_custom_call" | custom-call | tf_op jit(solution)/shard_map/pallas_call | solution.py:113
  23.6 0.0 copy-start.6
  23.6 1.3 copy-done.6
  24.9 0.0 copy-start.9
  24.9 0.6 copy-done.9
  25.5 8.2 %shard_map.79 = f32[8,8,256]{2,1,0:T(8,128)} custom-call(f32[8,256]{1,0:T(8,128)} %copy-done.9), custom_call_target="tpu_custom_call" | custom-call | tf_op jit(solution)/shard_map/pallas_call | solution.py:163
  33.8 1.1 slice_reduce_fusion.2
  34.9 2.9 %fusion.14 = (bf16[16,128,250]{2,1,0:T(8,128)(2,1)S(1)}, f32[16,128,250]{2,1,0:T(8,128)S(1)}, f32[16,128,250]{2,1,0:T(8,128)S(1)}) fusion(f32[32,128,250]{2,1,0:T(8,128)} %copy-done.13, f32[250]{0:T(256)S(1)} %div.52, f32[16,128,250]{2,1,0:T(8,128)} %copy-done.6, f32[250]{0:T(256)S(1)} %div.51), kind=kLoop, calls=%fused_computation.37 | loop fusion | flops 2560000 | bytes 9218000 | tf_op jit(solution)/shard_map/convert_element_type | solution.py:205
  37.8 0.0 copy-start.3
  37.8 23.2 %shard_map.80.blocks_ref = bf16[32,128,250]{2,1,0:T(8,128)(2,1)S(1)} custom-call(bf16[16,128,250]{2,1,0:T(8,128)(2,1)S(1)} %get-tuple-element.21.cells_ref), custom_call_target="tpu_custom_call" | custom-call | tf_op jit(solution)/shard_map/pallas_call | solution.py:51
  61.0 0.0 copy-start.1
  61.0 3.5 %copy-done.1 = bf16[16,17,128,128]{3,2,1,0:T(8,128)(2,1)S(1)} copy-done((bf16[16,17,128,128]{3,2,1,0:T(8,128)(2,1)S(1)}, bf16[16,17,128,128]{3,2,1,0:T(8,128)(2,1)}, u32[]{:S(2)}) %copy-start.1) | copy-done | bytes 8912920
  64.6 7.7 %shard_map.81 = (f32[16,128,250]{2,1,0:T(8,128)S(1)}, f32[8,256]{1,0:T(8,128)S(1)}) custom-call(s32[16,17]{1,0:T(8,128)S(1)} %fusion.2.index_ref, s32[16]{0:T(128)S(1)} %copy-done.12, bf16[16,17,128,128]{3,2,1,0:T(8,128)(2,1)S(1)} %copy-done.1, bf16[32,128,250]{2,1,0:T(8,128)(2,1)S(1)} %shard_map.80.blocks_ref, ...), custom_call_target="tpu_custom_call" | custom-call | tf_op jit(solution)/shard_map/pallas_call | solution.py:113
  72.3 0.0 copy-done.3
  72.3 0.0 copy-start.8
  72.3 1.3 copy-done.8
  73.6 0.6 copy-done.11
  74.2 8.3 %shard_map.82 = f32[8,8,256]{2,1,0:T(8,128)} custom-call(f32[8,256]{1,0:T(8,128)} %copy-done.11), custom_call_target="tpu_custom_call" | custom-call | tf_op jit(solution)/shard_map/pallas_call | solution.py:163
  82.5 1.0 slice_reduce_fusion.1
  83.6 3.0 %fusion.13 = (bf16[16,128,250]{2,1,0:T(8,128)(2,1)S(1)}, f32[16,128,250]{2,1,0:T(8,128)S(1)}, f32[16,128,250]{2,1,0:T(8,128)S(1)}) fusion(f32[16,128,250]{2,1,0:T(8,128)S(1)} %get-tuple-element.22.direction_ref, f32[250]{0:T(256)S(1)} %div.54, f32[16,128,250]{2,1,0:T(8,128)} %copy-done.3, f32[16,128,250]{2,1,0:T(8,128)} %copy-done.8, f32[250]{0:T(256)S(1)} %div.53), kind=kLoop, calls=%fused_computation.36 | loop fusion | flops 2560000 | bytes 11266000 | tf_op jit(solution)/shard_map/convert_element_type | solution.py:205
  86.6 0.0 copy-start.4
  86.6 0.0 copy-start.5
  86.6 24.2 %shard_map.83.blocks_ref = bf16[32,128,250]{2,1,0:T(8,128)(2,1)S(1)} custom-call(bf16[16,128,250]{2,1,0:T(8,128)(2,1)S(1)} %get-tuple-element.18.cells_ref), custom_call_target="tpu_custom_call" | custom-call | tf_op jit(solution)/shard_map/pallas_call | solution.py:51
  110.8 0.0 copy-start.2
  110.8 3.5 %copy-done.2 = bf16[16,17,128,128]{3,2,1,0:T(8,128)(2,1)S(1)} copy-done((bf16[16,17,128,128]{3,2,1,0:T(8,128)(2,1)S(1)}, bf16[16,17,128,128]{3,2,1,0:T(8,128)(2,1)}, u32[]{:S(2)}) %copy-start.2) | copy-done | bytes 8912920
  114.3 7.7 %shard_map.84 = (f32[16,128,250]{2,1,0:T(8,128)S(1)}, f32[8,256]{1,0:T(8,128)S(1)}) custom-call(s32[16,17]{1,0:T(8,128)S(1)} %fusion.2.index_ref, s32[16]{0:T(128)S(1)} %copy-done.12, bf16[16,17,128,128]{3,2,1,0:T(8,128)(2,1)S(1)} %copy-done.2, bf16[32,128,250]{2,1,0:T(8,128)(2,1)S(1)} %shard_map.83.blocks_ref, ...), custom_call_target="tpu_custom_call" | custom-call | tf_op jit(solution)/shard_map/pallas_call | solution.py:113
  122.0 0.0 copy-done.4
  122.0 0.0 copy-done.5
  122.1 0.0 copy-start.7
  122.1 1.3 copy-done.7
  123.4 0.6 copy-done.10
  124.0 8.6 %shard_map.85 = f32[8,8,256]{2,1,0:T(8,128)} custom-call(f32[8,256]{1,0:T(8,128)} %copy-done.10), custom_call_target="tpu_custom_call" | custom-call | tf_op jit(solution)/shard_map/pallas_call | solution.py:163
  132.6 0.9 slice_reduce_fusion
  133.5 6.6 %multiply_reduce_fusion = (f32[16,128]{1,0:T(8,128)}, f32[16,128,250]{2,1,0:T(8,128)}, f32[16,128,250]{2,1,0:T(8,128)}) fusion(f32[16,128,250]{2,1,0:T(8,128)} %copy-done.4, f32[250]{0:T(256)S(1)} %div.55, f32[16,128,250]{2,1,0:T(8,128)S(1)} %get-tuple-element.22.direction_ref, f32[250]{0:T(256)S(1)} %div.53, f32[32,128,250]{2,1,0:T(8,128)} %copy-done.13, ...), kind=kLoop, calls=%fused_computation.2 | loop fusion | flops 4605952 | bytes 14347192 | tf_op jit(solution)/shard_map/reduce_sum | solution.py:219
  140.1 5.0 %shard_map.86 = f32[4,16,128]{2,1,0:T(8,128)} custom-call(f32[16,128]{1,0:T(8,128)} %get-tuple-element.16.part_ref), custom_call_target="tpu_custom_call" | custom-call | tf_op jit(solution)/shard_map/pallas_call | solution.py:163
  145.1 0.8 reduce_sum.79
  145.9 3.3 %broadcast_divide_fusion = f32[16,128,250]{2,1,0:T(8,128)} fusion(f32[16,128,250]{2,1,0:T(8,128)} %get-tuple-element.17, f32[16,128]{1,0:T(8,128)S(1)} %add_sqrt_fusion), kind=kLoop, calls=%fused_computation.8 | loop fusion | flops 512000 | bytes 4104192 | tf_op jit(solution)/shard_map/div | solution.py:222
  (13 shorter events, 0.1 us)
Async XLA Ops:
  11.0 4.6 %copy-start = (bf16[16,17,128,128]{3,2,1,0:T(8,128)(2,1)S(1)}, bf16[16,17,128,128]{3,2,1,0:T(8,128)(2,1)}, u32[]{:S(2)}) copy-start(bf16[16,17,128,128]{3,2,1,0:T(8,128)(2,1)} %tiles_ref.5) | copy-start | bytes 26738692
  13.1 1.9 %copy-start.13 = (f32[32,128,250]{2,1,0:T(8,128)}, f32[32,128,250]{2,1,0:T(8,128)S(1)}, u32[]{:S(2)}) copy-start(f32[32,128,250]{2,1,0:T(8,128)S(1)} %get-tuple-element.32) | copy-start | bytes 12288004
  15.1 0.8 copy-start.12
  23.6 1.3 copy-start.6
  24.9 0.6 copy-start.9
  37.8 34.5 %copy-start.3 = (f32[16,128,250]{2,1,0:T(8,128)}, f32[16,128,250]{2,1,0:T(8,128)S(1)}, u32[]{:S(2)}) copy-start(f32[16,128,250]{2,1,0:T(8,128)S(1)} %get-tuple-element.23.residual_ref) | copy-start | bytes 6144004
  61.0 3.5 %copy-start.1 = (bf16[16,17,128,128]{3,2,1,0:T(8,128)(2,1)S(1)}, bf16[16,17,128,128]{3,2,1,0:T(8,128)(2,1)}, u32[]{:S(2)}) copy-start(bf16[16,17,128,128]{3,2,1,0:T(8,128)(2,1)} %tiles_ref.5) | copy-start | bytes 26738692
  72.3 1.3 copy-start.8
  73.6 0.6 copy-start.11
  86.6 35.5 %copy-start.4 = (f32[16,128,250]{2,1,0:T(8,128)}, f32[16,128,250]{2,1,0:T(8,128)S(1)}, u32[]{:S(2)}) copy-start(f32[16,128,250]{2,1,0:T(8,128)S(1)} %get-tuple-element.19.direction_ref) | copy-start | bytes 6144004
  86.6 35.5 %copy-start.5 = (f32[16,128,250]{2,1,0:T(8,128)}, f32[16,128,250]{2,1,0:T(8,128)S(1)}, u32[]{:S(2)}) copy-start(f32[16,128,250]{2,1,0:T(8,128)S(1)} %get-tuple-element.20.residual_ref) | copy-start | bytes 6144004
  110.8 3.5 %copy-start.2 = (bf16[16,17,128,128]{3,2,1,0:T(8,128)(2,1)S(1)}, bf16[16,17,128,128]{3,2,1,0:T(8,128)(2,1)}, u32[]{:S(2)}) copy-start(bf16[16,17,128,128]{3,2,1,0:T(8,128)(2,1)} %tiles_ref.5) | copy-start | bytes 26738692
  122.1 1.3 copy-start.7
  123.4 0.6 copy-start.10

commit v4 on v3

--- a/solution.py
+++ b/solution.py
@@ -57,7 +57,7 @@
         out_specs=pl.BlockSpec(memory_space=pltpu.VMEM),
         scratch_shapes=[pltpu.SemaphoreType.DMA((2,)), pltpu.SemaphoreType.DMA((2,))],
         compiler_params=pltpu.CompilerParams(
-            collective_id=collective_id, has_side_effects=True, vmem_limit_bytes=16 * 2**20
+            collective_id=collective_id, has_side_effects=True, vmem_limit_bytes=8 * 2**20
         ),
     )(cells)
 
@@ -127,7 +127,7 @@
             jax.ShapeDtypeStruct((rows, size, classes), jnp.float32),
             jax.ShapeDtypeStruct((8, lanes), jnp.float32),
         ],
-        compiler_params=pltpu.CompilerParams(vmem_limit_bytes=32 * 2**20),
+        compiler_params=pltpu.CompilerParams(vmem_limit_bytes=16 * 2**20),
     )(index, count, tiles, blocks, direction, residual)
 
 
@@ -167,7 +167,7 @@
         out_specs=pl.BlockSpec(memory_space=pltpu.VMEM),
         scratch_shapes=[pltpu.SemaphoreType.DMA((count,)), pltpu.SemaphoreType.DMA((count,))],
         compiler_params=pltpu.CompilerParams(
-            collective_id=collective_id, has_side_effects=True
+            collective_id=collective_id, has_side_effects=True, vmem_limit_bytes=2 * 2**20
         ),
     )(part)
 

time: 150 us -> 117 us (0.78)
  local copies, waits for them, and re-layouts: 15.6 us -> 1.46 us
  other arithmetic: 23.8 us -> 9.75 us
  Pallas kernels: 109 us -> 104 us
    unnamed x28 -> x4, local copies, waits for them, and re-layouts: 15.4 us -> 1.29 us
    pallas_call x4, Pallas kernels: 30.2 us -> 25.2 us  [gathered(): pl.pallas_call(functools.partial(gather_kernel, axis, count), out_shape=j...]
    convert_element_type x2, other arithmetic: 5.87 us -> 1.4 us  [body(): half = edges(direction.astype(jnp.bfloat16), half_span, 3)]
    reduce_sum x1, other arithmetic: 6.59 us -> 2.25 us  [body(): jnp.sum(solved * solved, axis=2)]
    reduce_sum x3, other arithmetic: 2.97 us -> 0.11 us  [body(): curve_sum = jnp.sum(parts[:, 0], axis=0)]
    div x1, other arithmetic: 3.26 us -> 1.67 us  [body(): return ((solved / length[:, :, None]).reshape(flat), residual.reshape(flat))]
where the time goes in v4:
time: 117 us; the launch traced here: 116 us
  Pallas kernels  104 us (89%)
  other arithmetic  9.75 us (8%)
  local copies, waits for them, and re-layouts  1.46 us (1%)
    pallas_call x3, Pallas kernels, edges(): pl.pallas_call(functools.partial(edges_kernel, width, lax.axis_size('rows...  55.5 us
    pallas_call x4, Pallas kernels, gathered(): pl.pallas_call(functools.partial(gather_kernel, axis, count), out_shape=j...  25.2 us
    pallas_call x3, Pallas kernels, product(): pl.pallas_call(product_kernel, grid_spec=pltpu.PrefetchScalarGridSpec(num...  23.4 us

profile of v4, /device:TPU:0, one launch (start us, length us, event | category | flops | bytes accessed | tf_op | source)
XLA Modules:
  0.0 116.2 jit_solution(9821870891843051776)
XLA Ops:
  0.6 0.7 fusion.2.index_ref
  1.4 0.7 convert_element_type.20
  2.1 0.7 pad_maximum_fusion.cells_ref
  2.8 8.2 %shard_map.77 = f32[32,2,128]{2,1,0:T(2,128)S(1)} custom-call(f32[16,2,128]{2,1,0:T(2,128)S(1)} %pad_maximum_fusion.cells_ref), custom_call_target="tpu_custom_call" | custom-call | tf_op jit(solution)/shard_map/pallas_call | solution.py:51
  11.0 0.0 copy-start
  11.0 2.1 %fusion = (bf16[32,128,250]{2,1,0:T(8,128)(2,1)S(1)}, f32[32,128,250]{2,1,0:T(8,128)S(1)}) fusion(f32[250]{0:T(256)S(1)} %add_convert_fusion, f32[32,128]{1,0:T(8,128)S(1)} %bitcast.45, f32[250]{0:T(256)} %param.11, f32[32,128]{1,0:T(8,128)S(1)} %bitcast.44), kind=kLoop, calls=%fused_computation.9 | loop fusion | flops 6144000 | bytes 6178768 | tf_op jit(solution)/shard_map/convert_element_type | solution.py:201
  13.1 0.0 copy-start.1
  13.2 0.1 slice.65.direction_ref.residual_ref
  13.3 1.3 %copy-done = bf16[16,17,128,128]{3,2,1,0:T(8,128)(2,1)S(1)} copy-done((bf16[16,17,128,128]{3,2,1,0:T(8,128)(2,1)S(1)}, bf16[16,17,128,128]{3,2,1,0:T(8,128)(2,1)}, u32[]{:S(2)}) %copy-start) | copy-done | bytes 8912920
  14.6 0.0 copy-done.1
  14.6 7.8 %shard_map.78 = (f32[16,128,250]{2,1,0:T(8,128)S(1)}, f32[8,256]{1,0:T(8,128)S(1)}) custom-call(s32[16,17]{1,0:T(8,128)S(1)} %fusion.2.index_ref, s32[16]{0:T(128)S(1)} %copy-done.1, bf16[16,17,128,128]{3,2,1,0:T(8,128)(2,1)S(1)} %copy-done, bf16[32,128,250]{2,1,0:T(8,128)(2,1)S(1)} %get-tuple-element.31.blocks_ref, ...), custom_call_target="tpu_custom_call" | custom-call | tf_op jit(solution)/shard_map/pallas_call | solution.py:113
  22.4 7.0 %shard_map.79 = f32[8,8,256]{2,1,0:T(8,128)S(1)} custom-call(f32[8,256]{1,0:T(8,128)S(1)} %get-tuple-element.8.part_ref), custom_call_target="tpu_custom_call" | custom-call | tf_op jit(solution)/shard_map/pallas_call | solution.py:163
  29.5 0.6 fusion.14
  30.1 23.1 %shard_map.80.blocks_ref = bf16[32,128,250]{2,1,0:T(8,128)(2,1)S(1)} custom-call(bf16[16,128,250]{2,1,0:T(8,128)(2,1)S(1)} %get-tuple-element.21.cells_ref), custom_call_target="tpu_custom_call" | custom-call | tf_op jit(solution)/shard_map/pallas_call | solution.py:51
  53.2 7.9 %shard_map.81 = (f32[16,128,250]{2,1,0:T(8,128)S(1)}, f32[8,256]{1,0:T(8,128)S(1)}) custom-call(s32[16,17]{1,0:T(8,128)S(1)} %fusion.2.index_ref, s32[16]{0:T(128)S(1)} %copy-done.1, bf16[16,17,128,128]{3,2,1,0:T(8,128)(2,1)S(1)} %copy-done, bf16[32,128,250]{2,1,0:T(8,128)(2,1)S(1)} %shard_map.80.blocks_ref, ...), custom_call_target="tpu_custom_call" | custom-call | tf_op jit(solution)/shard_map/pallas_call | solution.py:113
  61.1 7.1 %shard_map.82 = f32[8,8,256]{2,1,0:T(8,128)S(1)} custom-call(f32[8,256]{1,0:T(8,128)S(1)} %get-tuple-element.10.part_ref), custom_call_target="tpu_custom_call" | custom-call | tf_op jit(solution)/shard_map/pallas_call | solution.py:163
  68.3 0.8 fusion.13
  69.0 24.2 %shard_map.83.blocks_ref = bf16[32,128,250]{2,1,0:T(8,128)(2,1)S(1)} custom-call(bf16[16,128,250]{2,1,0:T(8,128)(2,1)S(1)} %get-tuple-element.18.cells_ref), custom_call_target="tpu_custom_call" | custom-call | tf_op jit(solution)/shard_map/pallas_call | solution.py:51
  93.3 7.7 %shard_map.84 = (f32[16,128,250]{2,1,0:T(8,128)S(1)}, f32[8,256]{1,0:T(8,128)S(1)}) custom-call(s32[16,17]{1,0:T(8,128)S(1)} %fusion.2.index_ref, s32[16]{0:T(128)S(1)} %copy-done.1, bf16[16,17,128,128]{3,2,1,0:T(8,128)(2,1)S(1)} %copy-done, bf16[32,128,250]{2,1,0:T(8,128)(2,1)S(1)} %shard_map.83.blocks_ref, ...), custom_call_target="tpu_custom_call" | custom-call | tf_op jit(solution)/shard_map/pallas_call | solution.py:113
  101.0 7.4 %shard_map.85 = f32[8,8,256]{2,1,0:T(8,128)S(1)} custom-call(f32[8,256]{1,0:T(8,128)S(1)} %get-tuple-element.12.part_ref), custom_call_target="tpu_custom_call" | custom-call | tf_op jit(solution)/shard_map/pallas_call | solution.py:163
  108.5 2.3 %multiply_reduce_fusion = (f32[16,128]{1,0:T(8,128)S(1)}, f32[16,128,250]{2,1,0:T(8,128)S(1)}, f32[16,128,250]{2,1,0:T(8,128)}) fusion(f32[16,128,250]{2,1,0:T(8,128)S(1)} %get-tuple-element.19.direction_ref, f32[250]{0:T(256)S(1)} %div.55, f32[16,128,250]{2,1,0:T(8,128)S(1)} %get-tuple-element.22.direction_ref, f32[250]{0:T(256)S(1)} %div.53, ...), kind=kLoop, calls=%fused_computation.2 | loop fusion | flops 4605952 | bytes 14347192 | tf_op jit(solution)/shard_map/reduce_sum | solution.py:219
  110.7 3.7 %shard_map.86 = f32[4,16,128]{2,1,0:T(8,128)S(1)} custom-call(f32[16,128]{1,0:T(8,128)S(1)} %get-tuple-element.16.part_ref), custom_call_target="tpu_custom_call" | custom-call | tf_op jit(solution)/shard_map/pallas_call | solution.py:163
  114.5 1.7 %broadcast_divide_fusion = f32[16,128,250]{2,1,0:T(8,128)} fusion(f32[16,128,250]{2,1,0:T(8,128)S(1)} %get-tuple-element.17, f32[16,128]{1,0:T(8,128)S(1)} %add_sqrt_fusion), kind=kLoop, calls=%fused_computation.8 | loop fusion | flops 512000 | bytes 4104192 | tf_op jit(solution)/shard_map/div | solution.py:222
  (14 shorter events, 0.2 us)
Async XLA Ops:
  11.0 3.5 %copy-start = (bf16[16,17,128,128]{3,2,1,0:T(8,128)(2,1)S(1)}, bf16[16,17,128,128]{3,2,1,0:T(8,128)(2,1)}, u32[]{:S(2)}) copy-start(bf16[16,17,128,128]{3,2,1,0:T(8,128)(2,1)} %tiles_ref.5) | copy-start | bytes 26738692
  13.1 1.4 %copy-start.1 = (s32[16]{0:T(128)S(1)}, s32[16]{0:T(128)}, u32[]{:S(2)}) copy-start(s32[16]{0:T(128)} %count_ref.5) | copy-start | bytes 196

commit v5 on v4

--- a/solution.py
+++ b/solution.py
@@ -63,60 +63,65 @@
 
 
 def product_kernel(index_ref, count_ref, tiles_ref, blocks_ref, direction_ref, residual_ref, image_ref, dots_ref):
-    row = pl.program_id(0)
+    together = tiles_ref.shape[0]
+    first = pl.program_id(0) * together
     slots = tiles_ref.shape[1]
-    live = count_ref[row]
-    lhs = jnp.concatenate([tiles_ref[0, k] for k in range(slots)], axis=1)
-    picked = []
-    for k in range(slots):
-        block = blocks_ref[index_ref[row, k]]
-        picked.append(jnp.where(k < live, block, jnp.zeros_like(block)))
-    rhs = jnp.concatenate(picked, axis=0)
-    total = jnp.dot(lhs, rhs, preferred_element_type=jnp.float32)
-    direction = direction_ref[0]
-    residual = residual_ref[0]
-    image = direction - damping * total
-    image_ref[0] = image
-
-    @pl.when(row == 0)
+
+    @pl.when(first == 0)
     def _():
         dots_ref[...] = jnp.zeros_like(dots_ref)
 
-    classes = image.shape[1]
-
-    def column(value):
-        return jnp.sum(value, axis=0, keepdims=True)
-
-    def held(at):
-        return dots_ref[at : at + 1, 0:classes]
-
-    weight = column(image * image)
-    best = column(residual * image) / jnp.where(weight > 0, weight, 1.0)
-    rest = residual - best * image
-    low = column(rest * rest)
-    mean, mass, least = held(1), held(2), held(4)
-    total_mass = mass + weight
-    share = weight / jnp.where(total_mass > 0, total_mass, 1.0)
-    gap = best - mean
-    dots_ref[0:1, 0:classes] = held(0) + column(direction * image)
-    dots_ref[1:2, 0:classes] = mean + gap * share
-    dots_ref[2:3, 0:classes] = total_mass
-    dots_ref[3:4, 0:classes] = held(3) + column(residual * residual)
-    dots_ref[4:5, 0:classes] = least + low + gap * gap * (mass * share)
+    for at in range(together):
+        row = first + at
+        live = count_ref[row]
+        lhs = jnp.concatenate([tiles_ref[at, k] for k in range(slots)], axis=1)
+        picked = []
+        for k in range(slots):
+            block = blocks_ref[index_ref[row, k]]
+            picked.append(jnp.where(k < live, block, jnp.zeros_like(block)))
+        rhs = jnp.concatenate(picked, axis=0)
+        total = jnp.dot(lhs, rhs, preferred_element_type=jnp.float32)
+        direction = direction_ref[at]
+        residual = residual_ref[at]
+        image = direction - damping * total
+        image_ref[at] = image
+
+        classes = image.shape[1]
+
+        def column(value):
+            return jnp.sum(value, axis=0, keepdims=True)
+
+        def held(line):
+            return dots_ref[line : line + 1, 0:classes]
+
+        weight = column(image * image)
+        best = column(residual * image) / jnp.where(weight > 0, weight, 1.0)
+        rest = residual - best * image
+        low = column(rest * rest)
+        mean, mass, least = held(1), held(2), held(4)
+        total_mass = mass + weight
+        share = weight / jnp.where(total_mass > 0, total_mass, 1.0)
+        gap = best - mean
+        dots_ref[0:1, 0:classes] = held(0) + column(direction * image)
+        dots_ref[1:2, 0:classes] = mean + gap * share
+        dots_ref[2:3, 0:classes] = total_mass
+        dots_ref[3:4, 0:classes] = held(3) + column(residual * residual)
+        dots_ref[4:5, 0:classes] = least + low + gap * gap * (mass * share)
 
 
 def product(index, count, tiles, blocks, direction, residual):
     rows, slots, size, _ = tiles.shape
     span, _, classes = blocks.shape
     lanes = pl.cdiv(classes, 128) * 128
-    by_row = pl.BlockSpec((1, size, classes), lambda i, a, b: (i, 0, 0))
+    together = 2 if rows % 2 == 0 else 1
+    by_row = pl.BlockSpec((together, size, classes), lambda i, a, b: (i, 0, 0))
     return pl.pallas_call(
         product_kernel,
         grid_spec=pltpu.PrefetchScalarGridSpec(
             num_scalar_prefetch=2,
-            grid=(rows,),
+            grid=(rows // together,),
             in_specs=[
-                pl.BlockSpec((1, slots, size, size), lambda i, a, b: (i, 0, 0, 0)),
+                pl.BlockSpec((together, slots, size, size), lambda i, a, b: (i, 0, 0, 0)),
                 pl.BlockSpec((span, size, classes), lambda i, a, b: (0, 0, 0)),
                 by_row,
                 by_row,

time: 117 us -> 110 us (0.940)
  Pallas kernels: 104 us -> 98 us
    pallas_call x3, Pallas kernels: 23.4 us -> 17.5 us  [product(): pl.pallas_call(product_kernel, grid_spec=pltpu.PrefetchScalarGridSpec(num...]
where the time goes in v5:
time: 110 us
  Pallas kernels  98 us (89%)
  other arithmetic  9.75 us (9%)
  local copies, waits for them, and re-layouts  1.46 us (1%)
    pallas_call x3, Pallas kernels, edges(): pl.pallas_call(functools.partial(edges_kernel, width, lax.axis_size('rows...  55.7 us
    pallas_call x4, Pallas kernels, gathered(): pl.pallas_call(functools.partial(gather_kernel, axis, count), out_shape=j...  24.8 us
    pallas_call x3, Pallas kernels, product(): pl.pallas_call(product_kernel, grid_spec=pltpu.PrefetchScalarGridSpec(num...  17.5 us
    reduce_sum x1, other arithmetic, body(): jnp.sum(solved * solved, axis=2)  2.25 us

profile of v5, /device:TPU:0, one launch (start us, length us, event | category | flops | bytes accessed | tf_op | source)
XLA Modules:
  0.0 110.0 jit_solution(3161612649265877638)
XLA Ops:
  0.6 0.7 fusion.2.index_ref
  1.4 0.7 convert_element_type.20
  2.1 0.7 pad_maximum_fusion.cells_ref
  2.8 8.2 %shard_map.77 = f32[32,2,128]{2,1,0:T(2,128)S(1)} custom-call(f32[16,2,128]{2,1,0:T(2,128)S(1)} %pad_maximum_fusion.cells_ref), custom_call_target="tpu_custom_call" | custom-call | tf_op jit(solution)/shard_map/pallas_call | solution.py:51
  11.0 0.0 copy-start
  11.0 2.1 %fusion = (bf16[32,128,250]{2,1,0:T(8,128)(2,1)S(1)}, f32[32,128,250]{2,1,0:T(8,128)S(1)}) fusion(f32[250]{0:T(256)S(1)} %add_convert_fusion, f32[32,128]{1,0:T(8,128)S(1)} %bitcast.45, f32[250]{0:T(256)} %param.11, f32[32,128]{1,0:T(8,128)S(1)} %bitcast.44), kind=kLoop, calls=%fused_computation.9 | loop fusion | flops 6144000 | bytes 6178768 | tf_op jit(solution)/shard_map/convert_element_type | solution.py:206
  13.1 0.0 copy-start.1
  13.2 0.1 slice.65.direction_ref.residual_ref
  13.3 1.3 %copy-done = bf16[16,17,128,128]{3,2,1,0:T(8,128)(2,1)S(1)} copy-done((bf16[16,17,128,128]{3,2,1,0:T(8,128)(2,1)S(1)}, bf16[16,17,128,128]{3,2,1,0:T(8,128)(2,1)}, u32[]{:S(2)}) %copy-start) | copy-done | bytes 8912920
  14.6 0.0 copy-done.1
  14.6 5.7 %shard_map.78 = (f32[16,128,250]{2,1,0:T(8,128)S(1)}, f32[8,256]{1,0:T(8,128)S(1)}) custom-call(s32[16,17]{1,0:T(8,128)S(1)} %fusion.2.index_ref, s32[16]{0:T(128)S(1)} %copy-done.1, bf16[16,17,128,128]{3,2,1,0:T(8,128)(2,1)S(1)} %copy-done, bf16[32,128,250]{2,1,0:T(8,128)(2,1)S(1)} %get-tuple-element.31.blocks_ref, ...), custom_call_target="tpu_custom_call" | custom-call | tf_op jit(solution)/shard_map/pallas_call | solution.py:118
  20.3 6.8 %shard_map.79 = f32[8,8,256]{2,1,0:T(8,128)S(1)} custom-call(f32[8,256]{1,0:T(8,128)S(1)} %get-tuple-element.8.part_ref), custom_call_target="tpu_custom_call" | custom-call | tf_op jit(solution)/shard_map/pallas_call | solution.py:168
  27.3 0.6 fusion.14
  27.9 23.3 %shard_map.80.blocks_ref = bf16[32,128,250]{2,1,0:T(8,128)(2,1)S(1)} custom-call(bf16[16,128,250]{2,1,0:T(8,128)(2,1)S(1)} %get-tuple-element.21.cells_ref), custom_call_target="tpu_custom_call" | custom-call | tf_op jit(solution)/shard_map/pallas_call | solution.py:51
  51.2 6.0 %shard_map.81 = (f32[16,128,250]{2,1,0:T(8,128)S(1)}, f32[8,256]{1,0:T(8,128)S(1)}) custom-call(s32[16,17]{1,0:T(8,128)S(1)} %fusion.2.index_ref, s32[16]{0:T(128)S(1)} %copy-done.1, bf16[16,17,128,128]{3,2,1,0:T(8,128)(2,1)S(1)} %copy-done, bf16[32,128,250]{2,1,0:T(8,128)(2,1)S(1)} %shard_map.80.blocks_ref, ...), custom_call_target="tpu_custom_call" | custom-call | tf_op jit(solution)/shard_map/pallas_call | solution.py:118
  57.3 6.9 %shard_map.82 = f32[8,8,256]{2,1,0:T(8,128)S(1)} custom-call(f32[8,256]{1,0:T(8,128)S(1)} %get-tuple-element.10.part_ref), custom_call_target="tpu_custom_call" | custom-call | tf_op jit(solution)/shard_map/pallas_call | solution.py:168
  64.2 0.8 fusion.13
  65.0 24.2 %shard_map.83.blocks_ref = bf16[32,128,250]{2,1,0:T(8,128)(2,1)S(1)} custom-call(bf16[16,128,250]{2,1,0:T(8,128)(2,1)S(1)} %get-tuple-element.18.cells_ref), custom_call_target="tpu_custom_call" | custom-call | tf_op jit(solution)/shard_map/pallas_call | solution.py:51
  89.2 5.7 %shard_map.84 = (f32[16,128,250]{2,1,0:T(8,128)S(1)}, f32[8,256]{1,0:T(8,128)S(1)}) custom-call(s32[16,17]{1,0:T(8,128)S(1)} %fusion.2.index_ref, s32[16]{0:T(128)S(1)} %copy-done.1, bf16[16,17,128,128]{3,2,1,0:T(8,128)(2,1)S(1)} %copy-done, bf16[32,128,250]{2,1,0:T(8,128)(2,1)S(1)} %shard_map.83.blocks_ref, ...), custom_call_target="tpu_custom_call" | custom-call | tf_op jit(solution)/shard_map/pallas_call | solution.py:118
  94.9 7.4 %shard_map.85 = f32[8,8,256]{2,1,0:T(8,128)S(1)} custom-call(f32[8,256]{1,0:T(8,128)S(1)} %get-tuple-element.12.part_ref), custom_call_target="tpu_custom_call" | custom-call | tf_op jit(solution)/shard_map/pallas_call | solution.py:168
  102.4 2.3 %multiply_reduce_fusion = (f32[16,128]{1,0:T(8,128)S(1)}, f32[16,128,250]{2,1,0:T(8,128)S(1)}, f32[16,128,250]{2,1,0:T(8,128)}) fusion(f32[16,128,250]{2,1,0:T(8,128)S(1)} %get-tuple-element.19.direction_ref, f32[250]{0:T(256)S(1)} %div.55, f32[16,128,250]{2,1,0:T(8,128)S(1)} %get-tuple-element.22.direction_ref, f32[250]{0:T(256)S(1)} %div.53, ...), kind=kLoop, calls=%fused_computation.2 | loop fusion | flops 4605952 | bytes 14347192 | tf_op jit(solution)/shard_map/reduce_sum | solution.py:224
  104.6 3.7 %shard_map.86 = f32[4,16,128]{2,1,0:T(8,128)S(1)} custom-call(f32[16,128]{1,0:T(8,128)S(1)} %get-tuple-element.16.part_ref), custom_call_target="tpu_custom_call" | custom-call | tf_op jit(solution)/shard_map/pallas_call | solution.py:168
  108.4 1.7 %broadcast_divide_fusion = f32[16,128,250]{2,1,0:T(8,128)} fusion(f32[16,128,250]{2,1,0:T(8,128)S(1)} %get-tuple-element.17, f32[16,128]{1,0:T(8,128)S(1)} %add_sqrt_fusion), kind=kLoop, calls=%fused_computation.8 | loop fusion | flops 512000 | bytes 4104192 | tf_op jit(solution)/shard_map/div | solution.py:227
  (14 shorter events, 0.2 us)
Async XLA Ops:
  11.0 3.5 %copy-start = (bf16[16,17,128,128]{3,2,1,0:T(8,128)(2,1)S(1)}, bf16[16,17,128,128]{3,2,1,0:T(8,128)(2,1)}, u32[]{:S(2)}) copy-start(bf16[16,17,128,128]{3,2,1,0:T(8,128)(2,1)} %tiles_ref.5) | copy-start | bytes 26738692
  13.1 1.4 %copy-start.1 = (s32[16]{0:T(128)S(1)}, s32[16]{0:T(128)}, u32[]{:S(2)}) copy-start(s32[16]{0:T(128)} %count_ref.5) | copy-start | bytes 196
